TPU v7x, 32 devices: a whole 2x2x4 slice. The times are simulated.
32 devices in a mesh: dp: 8 (over z, y), tensor: 4 (over x, core).
Axes of the slice: x: 2, y: 2, z: 4, core: 2. Of those that a mesh axis runs over, the one named last changes fastest.
Arguments:
- layer_input: bfloat16 [4096, 2560], P(('dp', 'tensor')), may hold values from -6 to 6
- doc_ids: int32 [4096], P('dp'), may hold values from 0 to 4, as said below
- norm_in: bfloat16 [2, 2560], P(None, 'dp'), may hold values from 0.5 to 1.5
- q_down: bfloat16 [2, 2560, 768], P(None, 'dp'), may hold values from -0.125 to 0.125
- q_gain: bfloat16 [2, 768], P(None, 'dp'), may hold values from 0.5 to 1.5
- q_up: bfloat16 [2, 768, 3840], P(None, 'dp', 'tensor'), may hold values from -0.21875 to 0.21875
- kv_down: bfloat16 [2, 2560, 288], P(None, 'dp'), may hold values from -0.125 to 0.125
- kv_gain: bfloat16 [2, 256], P(None, 'dp'), may hold values from 0.5 to 1.5
- kv_up: bfloat16 [2, 256, 5120], P(None, 'dp', 'tensor'), may hold values from -0.375 to 0.375
- out_proj: bfloat16 [2, 2560, 2560], P(None, 'tensor', 'dp'), may hold values from -2 to 2
- norm_post: bfloat16 [2, 2560], P(None, 'dp'), may hold values from 0.5 to 1.5
- gate_proj: bfloat16 [2, 2560, 6400], P(None, 'dp', 'tensor'), may hold values from -0.125 to 0.125
- up_proj: bfloat16 [2, 2560, 6400], P(None, 'dp', 'tensor'), may hold values from -0.125 to 0.125
- down_proj: bfloat16 [2, 6400, 2560], P(None, 'tensor', 'dp'), may hold values from -0.375 to 0.375
- out_grad: bfloat16 [4096, 2560], P(('dp', 'tensor')), may hold values from -6 to 6
Outputs:
- layer_output: bfloat16 [4096, 2560], P(('dp', 'tensor'))
- input_grad: bfloat16 [4096, 2560], P(('dp', 'tensor'))
- grad_norm_in: float32 [2, 2560], P(None, 'dp')
- grad_q_down: float32 [2, 2560, 768], P(None, 'dp')
- grad_q_gain: float32 [2, 768], P(None, 'dp')
- grad_q_up: float32 [2, 768, 3840], P(None, 'dp', 'tensor')
- grad_kv_down: float32 [2, 2560, 288], P(None, 'dp')
- grad_kv_gain: float32 [2, 256], P(None, 'dp')
- grad_kv_up: float32 [2, 256, 5120], P(None, 'dp', 'tensor')
- grad_out_proj: float32 [2, 2560, 2560], P(None, 'tensor', 'dp')
- grad_norm_post: float32 [2, 2560], P(None, 'dp')
- grad_gate_proj: float32 [2, 2560, 6400], P(None, 'dp', 'tensor')
- grad_up_proj: float32 [2, 2560, 6400], P(None, 'dp', 'tensor')
- grad_down_proj: float32 [2, 6400, 2560], P(None, 'tensor', 'dp')
Inputs may be any that keep to these rules, and one draw needn't show every extreme that they name: `doc_ids`: within each group of 512 rows (one index of dp) the ids start at 0 and rise by 0 or 1 from row to row, ending at 4; rows with equal ids form one document.
All inputs are finite; a program needn't handle non-finite values.
Results may differ from a plain program's by a relative error of at most 0.035.
Values may be sent and summed in bfloat16 or wider, within the bound.
No kernel may reach another device: no remote copies, remote signals or barrier semaphores. Data moves between devices by JAX's collectives and lax.ppermute only.
A program may use at most 320 MiB of HBM per device.

v0:
```python
import math

import jax
import jax.numpy as jnp
from jax import lax
from jax.sharding import PartitionSpec as P

NOPE = 64
ROPE = 32
VDIM = 64
KVR = 256
LAYERS = 2
QK = 96


epsilon = 1e-05
residual_scale = 1.4 / math.sqrt(62.0)
rope_base = 10000.0
masked_score = -1e30


def norm_parts(values):
    inverse = lax.rsqrt(jnp.mean(values * values, axis=-1, keepdims=True) + epsilon)
    return (values * inverse, inverse)


def norm_back(normed, inverse, gain, upstream):
    scaled = upstream * gain
    result = inverse * (scaled - normed * jnp.mean(scaled * normed, axis=-1, keepdims=True))
    return (result, jnp.sum(upstream * normed, axis=0))


def rotate(rotary, cosine, sine_table):
    half_width = rotary.shape[-1] // 2
    first_half = rotary[..., :half_width]
    second_half = rotary[..., half_width:]
    return jnp.concatenate(
        [
            first_half * cosine - second_half * sine_table,
            second_half * cosine + first_half * sine_table,
        ],
        axis=-1,
    )


def rotate_back(upstream, cosine, sine_table):
    half_width = upstream.shape[-1] // 2
    first_half = upstream[..., :half_width]
    second_half = upstream[..., half_width:]
    return jnp.concatenate(
        [
            first_half * cosine + second_half * sine_table,
            second_half * cosine - first_half * sine_table,
        ],
        axis=-1,
    )


def tables(doc_ids):
    rows_total = doc_ids.shape[0]
    places = jnp.arange(rows_total, dtype=jnp.int32)
    begins = jnp.concatenate([jnp.ones((1,), dtype=bool), doc_ids[1:] != doc_ids[:-1]])
    starts = lax.cummax(jnp.where(begins, places, 0), axis=0)
    positions = (places - starts).astype(jnp.float32)
    frequency = rope_base ** (-jnp.arange(0, ROPE, 2, dtype=jnp.float32) / ROPE)
    angles = positions[:, None] * frequency[None, :]
    allowed = (doc_ids[:, None] == doc_ids[None, :]) & (places[:, None] >= places[None, :])
    return (jnp.cos(angles), jnp.sin(angles), allowed)


def gather_layer(stacks, layer_index):
    return (
        lax.all_gather(stacks[0][layer_index], "dp", axis=0, tiled=True),
        lax.all_gather(stacks[1][layer_index], "dp", axis=0, tiled=True),
        lax.all_gather(stacks[2][layer_index], "dp", axis=0, tiled=True),
        lax.all_gather(stacks[3][layer_index], "dp", axis=0, tiled=True),
        lax.all_gather(stacks[4][layer_index], "dp", axis=0, tiled=True),
        lax.all_gather(stacks[5][layer_index], "dp", axis=0, tiled=True),
        lax.all_gather(stacks[6][layer_index], "dp", axis=0, tiled=True),
        lax.all_gather(stacks[7][layer_index], "dp", axis=1, tiled=True),
        lax.all_gather(stacks[8][layer_index], "dp", axis=0, tiled=True),
        lax.all_gather(stacks[9][layer_index], "dp", axis=0, tiled=True),
        lax.all_gather(stacks[10][layer_index], "dp", axis=0, tiled=True),
        lax.all_gather(stacks[11][layer_index], "dp", axis=1, tiled=True),
    )


def spread_rows(rows_low):
    return lax.all_gather(rows_low, "tensor", axis=0, tiled=True)


def collect_rows(partial_rows):
    return lax.psum_scatter(
        partial_rows.astype(jnp.bfloat16), "tensor", scatter_dimension=0, tiled=True
    ).astype(jnp.float32)


def spread_grads(grads_low):
    return lax.all_gather(grads_low, "tensor", axis=0, tiled=True)


def block_shape(rows_total):
    block_rows = min(rows_total, 512)
    return (block_rows, rows_total // block_rows)


def block_scores(query_block, key_rows, mask_block, scale_factor):
    scores = (
        jnp.einsum("qhd,khd->hqk", query_block, key_rows, preferred_element_type=jnp.float32)
        * scale_factor
    )
    return jnp.where(mask_block[None], scores, masked_score)


def attend_forward(queries, key_rows, values, allowed, scale_factor):
    rows_total, heads_local, head_width = queries.shape
    block_rows, blocks = block_shape(rows_total)

    def one_block(inputs):
        query_block, mask_block = inputs
        scores = block_scores(query_block, key_rows, mask_block, scale_factor)
        highest = jnp.max(scores, axis=-1, keepdims=True)
        expanded = jnp.exp(scores - highest)
        totals = jnp.sum(expanded, axis=-1, keepdims=True)
        probs_low = (expanded / totals).astype(jnp.bfloat16)
        attended = jnp.einsum("hqk,khd->qhd", probs_low, values, preferred_element_type=jnp.float32)
        return (attended, (highest + jnp.log(totals))[..., 0])

    attended, log_totals = lax.map(
        one_block,
        (
            queries.reshape(blocks, block_rows, heads_local, head_width),
            allowed.reshape(blocks, block_rows, rows_total),
        ),
    )
    return (attended.reshape(rows_total, heads_local, values.shape[2]), log_totals)


def attend_backward(queries, key_rows, values, allowed, log_totals, att_grad, scale_factor):
    rows_total, heads_local, head_width = queries.shape
    block_rows, blocks = block_shape(rows_total)

    def one_block(carried, inputs):
        key_grad, value_grad = carried
        query_block, mask_block, log_block, grad_block = inputs
        scores = block_scores(query_block, key_rows, mask_block, scale_factor)
        probability = jnp.exp(scores - log_block[..., None])
        probs_low = probability.astype(jnp.bfloat16)
        value_grad = value_grad + jnp.einsum(
            "hqk,qhd->khd", probs_low, grad_block, preferred_element_type=jnp.float32
        )
        prob_grad = jnp.einsum(
            "qhd,khd->hqk", grad_block, values, preferred_element_type=jnp.float32
        )
        inner_sum = jnp.sum(prob_grad * probability, axis=-1, keepdims=True)
        score_grad = (probability * (prob_grad - inner_sum)).astype(jnp.bfloat16)
        query_grad = (
            jnp.einsum("hqk,khd->qhd", score_grad, key_rows, preferred_element_type=jnp.float32)
            * scale_factor
        )
        key_grad = (
            key_grad
            + jnp.einsum(
                "hqk,qhd->khd", score_grad, query_block, preferred_element_type=jnp.float32
            )
            * scale_factor
        )
        return ((key_grad, value_grad), query_grad)

    initial = (
        jnp.zeros((rows_total, heads_local, head_width), jnp.float32),
        jnp.zeros((rows_total, heads_local, values.shape[2]), jnp.float32),
    )
    inputs = (
        queries.reshape(blocks, block_rows, heads_local, head_width),
        allowed.reshape(blocks, block_rows, rows_total),
        log_totals,
        att_grad.reshape(blocks, block_rows, heads_local, values.shape[2]),
    )
    (key_grad, value_grad), query_grad = lax.scan(one_block, initial, inputs)
    return (query_grad.reshape(rows_total, heads_local, head_width), key_grad, value_grad)


def layer_forward(rows_in, weights, cosine, sine_table, allowed):
    (
        gain_in,
        q_down_w,
        q_gain_w,
        q_up_w,
        kv_down_w,
        kv_gain_w,
        kv_up_w,
        out_w,
        gain_post,
        gate_w,
        up_w,
        down_w,
    ) = weights
    rows_total = allowed.shape[0]
    heads_local = q_up_w.shape[1] // QK
    scale_factor = 1.0 / math.sqrt(QK)
    normed_in, inv_in = norm_parts(rows_in)
    low_in = (normed_in * gain_in.astype(jnp.float32)).astype(jnp.bfloat16)
    all_in = spread_rows(low_in)
    q_latent = jnp.dot(all_in, q_down_w, preferred_element_type=jnp.float32)
    q_normed, q_inverse = norm_parts(q_latent)
    q_low = (q_normed * q_gain_w.astype(jnp.float32)).astype(jnp.bfloat16)
    q_full = jnp.dot(q_low, q_up_w, preferred_element_type=jnp.float32).reshape(
        rows_total, heads_local, QK
    )
    kv_latent = jnp.dot(all_in, kv_down_w, preferred_element_type=jnp.float32)
    kv_normed, kv_inverse = norm_parts(kv_latent[:, :KVR])
    kv_low = (kv_normed * kv_gain_w.astype(jnp.float32)).astype(jnp.bfloat16)
    kv_full = jnp.dot(kv_low, kv_up_w, preferred_element_type=jnp.float32).reshape(
        rows_total, heads_local, NOPE + VDIM
    )
    queries = jnp.concatenate(
        [
            q_full[..., :NOPE],
            rotate(q_full[..., NOPE:], cosine[:, None, :], sine_table[:, None, :]),
        ],
        axis=-1,
    ).astype(jnp.bfloat16)
    shared = rotate(kv_latent[:, KVR:], cosine, sine_table)
    key_rows = jnp.concatenate(
        [
            kv_full[..., :NOPE],
            jnp.broadcast_to(shared[:, None, :], (rows_total, heads_local, ROPE)),
        ],
        axis=-1,
    ).astype(jnp.bfloat16)
    values = kv_full[..., NOPE:].astype(jnp.bfloat16)
    attended, log_totals = attend_forward(queries, key_rows, values, allowed, scale_factor)
    att_low = attended.reshape(rows_total, heads_local * VDIM).astype(jnp.bfloat16)
    middle = rows_in + residual_scale * collect_rows(
        jnp.dot(att_low, out_w, preferred_element_type=jnp.float32)
    )
    normed_mid, inv_mid = norm_parts(middle)
    low_mid = (normed_mid * gain_post.astype(jnp.float32)).astype(jnp.bfloat16)
    all_mid = spread_rows(low_mid)
    gate_act = jnp.dot(all_mid, gate_w, preferred_element_type=jnp.float32)
    up_act = jnp.dot(all_mid, up_w, preferred_element_type=jnp.float32)
    hidden = (jax.nn.silu(gate_act) * up_act).astype(jnp.bfloat16)
    result = middle + residual_scale * collect_rows(
        jnp.dot(hidden, down_w, preferred_element_type=jnp.float32)
    )
    stored = (
        normed_in,
        inv_in,
        low_in,
        q_normed,
        q_inverse,
        q_low,
        kv_normed,
        kv_inverse,
        kv_low,
        queries,
        key_rows,
        values,
        log_totals,
        att_low,
        normed_mid,
        inv_mid,
        all_mid,
        gate_act,
        up_act,
        hidden,
    )
    return (result, stored)


def own_slice(source, offset, own_rows):
    return lax.dynamic_slice_in_dim(source, offset, own_rows, 0)


def layer_backward(grad_rows, weights, stored, cosine, sine_table, allowed):
    (
        gain_in,
        q_down_w,
        q_gain_w,
        q_up_w,
        kv_down_w,
        kv_gain_w,
        kv_up_w,
        out_w,
        gain_post,
        gate_w,
        up_w,
        down_w,
    ) = weights
    (
        normed_in,
        inv_in,
        low_in,
        q_normed,
        q_inverse,
        q_low,
        kv_normed,
        kv_inverse,
        kv_low,
        queries,
        key_rows,
        values,
        log_totals,
        att_low,
        normed_mid,
        inv_mid,
        all_mid,
        gate_act,
        up_act,
        hidden,
    ) = stored
    rows_total = allowed.shape[0]
    heads_local = q_up_w.shape[1] // QK
    scale_factor = 1.0 / math.sqrt(QK)
    own_rows = grad_rows.shape[0]
    offset = lax.axis_index("tensor") * own_rows
    branch_two = spread_grads((residual_scale * grad_rows).astype(jnp.bfloat16))
    grad_down = jnp.einsum("rf,rd->fd", hidden, branch_two, preferred_element_type=jnp.float32)
    grad_hidden = jnp.einsum("rd,fd->rf", branch_two, down_w, preferred_element_type=jnp.float32)
    logistic = jax.nn.sigmoid(gate_act)
    grad_gate_low = (grad_hidden * up_act * logistic * (1.0 + gate_act * (1.0 - logistic))).astype(
        jnp.bfloat16
    )
    grad_up_low = (grad_hidden * gate_act * logistic).astype(jnp.bfloat16)
    grad_gate = jnp.einsum("rd,rf->df", all_mid, grad_gate_low, preferred_element_type=jnp.float32)
    grad_up = jnp.einsum("rd,rf->df", all_mid, grad_up_low, preferred_element_type=jnp.float32)
    mid_partial = jnp.einsum(
        "rf,df->rd", grad_gate_low, gate_w, preferred_element_type=jnp.float32
    ) + jnp.einsum("rf,df->rd", grad_up_low, up_w, preferred_element_type=jnp.float32)
    mid_grad = lax.psum_scatter(
        mid_partial.astype(jnp.bfloat16), "tensor", scatter_dimension=0, tiled=True
    ).astype(jnp.float32)
    back_mid, grad_gain_post = norm_back(
        normed_mid, inv_mid, gain_post.astype(jnp.float32), mid_grad
    )
    grad_middle = grad_rows + back_mid
    branch_one = spread_grads((residual_scale * grad_middle).astype(jnp.bfloat16))
    grad_out = jnp.einsum("rk,rd->kd", att_low, branch_one, preferred_element_type=jnp.float32)
    att_grad = jnp.einsum(
        "rd,kd->rk", branch_one, out_w, preferred_element_type=jnp.float32
    ).astype(jnp.bfloat16)
    query_grad, key_grad, value_grad = attend_backward(
        queries,
        key_rows,
        values,
        allowed,
        log_totals,
        att_grad.reshape(rows_total, heads_local, VDIM),
        scale_factor,
    )
    q_full_grad = (
        jnp.concatenate(
            [
                query_grad[..., :NOPE],
                rotate_back(query_grad[..., NOPE:], cosine[:, None, :], sine_table[:, None, :]),
            ],
            axis=-1,
        )
        .astype(jnp.bfloat16)
        .reshape(rows_total, heads_local * QK)
    )
    shared_grad = jnp.sum(
        rotate_back(key_grad[..., NOPE:], cosine[:, None, :], sine_table[:, None, :]), axis=1
    )
    kv_full_grad = (
        jnp.concatenate([key_grad[..., :NOPE], value_grad], axis=-1)
        .astype(jnp.bfloat16)
        .reshape(rows_total, heads_local * (NOPE + VDIM))
    )
    grad_q_up = jnp.einsum("rc,rk->ck", q_low, q_full_grad, preferred_element_type=jnp.float32)
    grad_kv_up = jnp.einsum("rc,rk->ck", kv_low, kv_full_grad, preferred_element_type=jnp.float32)
    q_norm_part = jnp.einsum("rk,ck->rc", q_full_grad, q_up_w, preferred_element_type=jnp.float32)
    kv_norm_part = jnp.einsum(
        "rk,ck->rc", kv_full_grad, kv_up_w, preferred_element_type=jnp.float32
    )
    q_norm_grad, kv_norm_grad, shared_own = (
        lax.psum_scatter(
            q_norm_part.astype(jnp.bfloat16), "tensor", scatter_dimension=0, tiled=True
        ).astype(jnp.float32),
        lax.psum_scatter(
            kv_norm_part.astype(jnp.bfloat16), "tensor", scatter_dimension=0, tiled=True
        ).astype(jnp.float32),
        lax.psum_scatter(
            shared_grad.astype(jnp.bfloat16), "tensor", scatter_dimension=0, tiled=True
        ).astype(jnp.float32),
    )
    q_latent_grad, grad_q_gain = norm_back(
        own_slice(q_normed, offset, own_rows),
        own_slice(q_inverse, offset, own_rows),
        q_gain_w.astype(jnp.float32),
        q_norm_grad,
    )
    q_latent_low = q_latent_grad.astype(jnp.bfloat16)
    kv_part_grad, grad_kv_gain = norm_back(
        own_slice(kv_normed, offset, own_rows),
        own_slice(kv_inverse, offset, own_rows),
        kv_gain_w.astype(jnp.float32),
        kv_norm_grad,
    )
    kv_latent_low = jnp.concatenate([kv_part_grad, shared_own], axis=-1).astype(jnp.bfloat16)
    grad_q_down = jnp.einsum("rd,rc->dc", low_in, q_latent_low, preferred_element_type=jnp.float32)
    grad_kv_down = jnp.einsum(
        "rd,rc->dc", low_in, kv_latent_low, preferred_element_type=jnp.float32
    )
    in_grad = jnp.einsum(
        "rc,dc->rd", q_latent_low, q_down_w, preferred_element_type=jnp.float32
    ) + jnp.einsum("rc,dc->rd", kv_latent_low, kv_down_w, preferred_element_type=jnp.float32)
    back_in, grad_gain_in = norm_back(normed_in, inv_in, gain_in.astype(jnp.float32), in_grad)
    grads = (
        grad_gain_in,
        grad_q_down,
        grad_q_gain,
        grad_q_up,
        grad_kv_down,
        grad_kv_gain,
        grad_kv_up,
        grad_out,
        grad_gain_post,
        grad_gate,
        grad_up,
        grad_down,
    )
    return (grad_middle + back_in, grads)


def body(
    layer_input,
    doc_ids,
    norm_in,
    q_down,
    q_gain,
    q_up,
    kv_down,
    kv_gain,
    kv_up,
    out_proj,
    norm_post,
    gate_proj,
    up_proj,
    down_proj,
    out_grad,
):
    stacks = (
        norm_in,
        q_down,
        q_gain,
        q_up,
        kv_down,
        kv_gain,
        kv_up,
        out_proj,
        norm_post,
        gate_proj,
        up_proj,
        down_proj,
    )
    cosine, sine_table, allowed = tables(doc_ids)
    current = layer_input.astype(jnp.float32)
    kept_weights = []
    stored_all = []
    for layer_index in range(LAYERS):
        weights = gather_layer(stacks, layer_index)
        current, stored = layer_forward(current, weights, cosine, sine_table, allowed)
        kept_weights.append(weights)
        stored_all.append(stored)
    grad_rows = out_grad.astype(jnp.float32)
    layer_grads = [None] * LAYERS
    for layer_index in reversed(range(LAYERS)):
        weights = gather_layer(stacks, layer_index)
        grad_rows, grads = layer_backward(
            grad_rows, weights, stored_all[layer_index], cosine, sine_table, allowed
        )
        sharded = (
            lax.psum_scatter(
                grads[0].astype(jnp.bfloat16), "dp", scatter_dimension=0, tiled=True
            ).astype(jnp.float32),
            lax.psum_scatter(
                grads[1].astype(jnp.bfloat16), "dp", scatter_dimension=0, tiled=True
            ).astype(jnp.float32),
            lax.psum_scatter(
                grads[2].astype(jnp.bfloat16), "dp", scatter_dimension=0, tiled=True
            ).astype(jnp.float32),
            lax.psum_scatter(
                grads[3].astype(jnp.bfloat16), "dp", scatter_dimension=0, tiled=True
            ).astype(jnp.float32),
            lax.psum_scatter(
                grads[4].astype(jnp.bfloat16), "dp", scatter_dimension=0, tiled=True
            ).astype(jnp.float32),
            lax.psum_scatter(
                grads[5].astype(jnp.bfloat16), "dp", scatter_dimension=0, tiled=True
            ).astype(jnp.float32),
            lax.psum_scatter(
                grads[6].astype(jnp.bfloat16), "dp", scatter_dimension=0, tiled=True
            ).astype(jnp.float32),
            lax.psum_scatter(
                grads[7].astype(jnp.bfloat16), "dp", scatter_dimension=1, tiled=True
            ).astype(jnp.float32),
            lax.psum_scatter(
                grads[8].astype(jnp.bfloat16), "dp", scatter_dimension=0, tiled=True
            ).astype(jnp.float32),
            lax.psum_scatter(
                grads[9].astype(jnp.bfloat16), "dp", scatter_dimension=0, tiled=True
            ).astype(jnp.float32),
            lax.psum_scatter(
                grads[10].astype(jnp.bfloat16), "dp", scatter_dimension=0, tiled=True
            ).astype(jnp.float32),
            lax.psum_scatter(
                grads[11].astype(jnp.bfloat16), "dp", scatter_dimension=1, tiled=True
            ).astype(jnp.float32),
        )
        summed = (
            lax.psum(sharded[0].astype(jnp.bfloat16), "tensor").astype(jnp.float32),
            lax.psum(sharded[1].astype(jnp.bfloat16), "tensor").astype(jnp.float32),
            lax.psum(sharded[2].astype(jnp.bfloat16), "tensor").astype(jnp.float32),
            lax.psum(sharded[4].astype(jnp.bfloat16), "tensor").astype(jnp.float32),
            lax.psum(sharded[5].astype(jnp.bfloat16), "tensor").astype(jnp.float32),
            lax.psum(sharded[8].astype(jnp.bfloat16), "tensor").astype(jnp.float32),
        )
        layer_grads[layer_index] = (
            summed[0],
            summed[1],
            summed[2],
            sharded[3],
            summed[3],
            summed[4],
            sharded[6],
            sharded[7],
            summed[5],
            sharded[9],
            sharded[10],
            sharded[11],
        )
    outputs = tuple(
        (jnp.stack([per_layer[position] for per_layer in layer_grads]) for position in range(12))
    )
    return (current.astype(jnp.bfloat16), grad_rows.astype(jnp.bfloat16)) + outputs


def solution(mesh):
    in_specs = (
        P(("dp", "tensor"), None),
        P("dp"),
        P(None, "dp"),
        P(None, "dp", None),
        P(None, "dp"),
        P(None, "dp", "tensor"),
        P(None, "dp", None),
        P(None, "dp"),
        P(None, "dp", "tensor"),
        P(None, "tensor", "dp"),
        P(None, "dp"),
        P(None, "dp", "tensor"),
        P(None, "dp", "tensor"),
        P(None, "tensor", "dp"),
        P(("dp", "tensor"), None),
    )
    out_specs = (
        P(("dp", "tensor"), None),
        P(("dp", "tensor"), None),
        P(None, "dp"),
        P(None, "dp", None),
        P(None, "dp"),
        P(None, "dp", "tensor"),
        P(None, "dp", None),
        P(None, "dp"),
        P(None, "dp", "tensor"),
        P(None, "tensor", "dp"),
        P(None, "dp"),
        P(None, "dp", "tensor"),
        P(None, "dp", "tensor"),
        P(None, "tensor", "dp"),
    )
    return jax.shard_map(body, mesh=mesh, in_specs=in_specs, out_specs=out_specs, check_vma=False)
```

profile of v0, /device:TPU:0, one launch (start us, length us, event | category | flops | bytes accessed | tf_op | source)
XLA Modules:
  0.0 3734.9 jit_solution(12175642043529031205)
XLA Ops:
  129.3 64.7 %all-gather.65.cloned.1.call-done = bf16[1,2560,768]{2,1,0:T(8,128)(2,1)} async-done(((bf16[1,320,768]{2,1,0:T(8,128)(2,1)}), bf16[1,2560,768]{2,1,0:T(8,128)(2,1)}) %all-gather.65.cloned.1.call-update) | async-done | bytes 3932176 | tf_op jit(solution)/shard_map/all_gather | solution.py:74
  251.8 50.7 %all-gather.69.cloned.1.call-done = bf16[1,640,2560]{1,2,0:T(8,128)(2,1)} async-done(((bf16[1,640,320]{1,2,0:T(8,128)(2,1)}), bf16[1,640,2560]{1,2,0:T(8,128)(2,1)}) %all-gather.69.cloned.1.call-update) | async-done | bytes 3276816 | tf_op jit(solution)/shard_map/all_gather | solution.py:80
  352.1 119.1 %all-gather.71.cloned.1.call-done = bf16[1,2560,1600]{2,1,0:T(8,128)(2,1)} async-done(((bf16[1,320,1600]{2,1,0:T(8,128)(2,1)}), bf16[1,2560,1600]{2,1,0:T(8,128)(2,1)}) %all-gather.71.cloned.1.call-update) | async-done | bytes 8192016 | tf_op jit(solution)/shard_map/all_gather | solution.py:82
  507.6 119.3 %all-gather.73.cloned.1.call-done = bf16[1,2560,1600]{2,1,0:T(8,128)(2,1)} async-done(((bf16[1,320,1600]{2,1,0:T(8,128)(2,1)}), bf16[1,2560,1600]{2,1,0:T(8,128)(2,1)}) %all-gather.73.cloned.1.call-update) | async-done | bytes 8192016 | tf_op jit(solution)/shard_map/all_gather | solution.py:83
  639.2 115.4 %all-gather.75.cloned.1.call-done = bf16[1,1600,2560]{1,2,0:T(8,128)(2,1)} async-done(((bf16[1,1600,320]{1,2,0:T(8,128)(2,1)}), bf16[1,1600,2560]{1,2,0:T(8,128)(2,1)}) %all-gather.75.cloned.1.call-update) | async-done | bytes 8192016 | tf_op jit(solution)/shard_map/all_gather | solution.py:84
  909.5 63.5 %all-gather.79.cloned.1.call-done = bf16[1,2560,768]{2,1,0:T(8,128)(2,1)} async-done(((bf16[1,320,768]{2,1,0:T(8,128)(2,1)}), bf16[1,2560,768]{2,1,0:T(8,128)(2,1)}) %all-gather.79.cloned.1.call-update) | async-done | bytes 3932176 | tf_op jit(solution)/shard_map/all_gather | solution.py:74
  1030.9 49.6 %all-gather.83.cloned.1.call-done = bf16[1,640,2560]{1,2,0:T(8,128)(2,1)} async-done(((bf16[1,640,320]{1,2,0:T(8,128)(2,1)}), bf16[1,640,2560]{1,2,0:T(8,128)(2,1)}) %all-gather.83.cloned.1.call-update) | async-done | bytes 3276816 | tf_op jit(solution)/shard_map/all_gather | solution.py:80
  1147.5 129.1 %all-gather.89.cloned.1.call-done = bf16[1,1600,2560]{1,2,0:T(8,128)(2,1)} async-done(((bf16[1,1600,320]{1,2,0:T(8,128)(2,1)}), bf16[1,1600,2560]{1,2,0:T(8,128)(2,1)}) %all-gather.89.cloned.1.call-update) | async-done | bytes 8192016 | tf_op jit(solution)/shard_map/all_gather | solution.py:84
  1287.0 116.7 %all-gather.87.cloned.1.call-done = bf16[1,2560,1600]{2,1,0:T(8,128)(2,1)} async-done(((bf16[1,320,1600]{2,1,0:T(8,128)(2,1)}), bf16[1,2560,1600]{2,1,0:T(8,128)(2,1)}) %all-gather.87.cloned.1.call-update) | async-done | bytes 8192016 | tf_op jit(solution)/shard_map/all_gather | solution.py:83
  1439.5 118.7 %all-gather.85.cloned.1.call-done = bf16[1,2560,1600]{2,1,0:T(8,128)(2,1)} async-done(((bf16[1,320,1600]{2,1,0:T(8,128)(2,1)}), bf16[1,2560,1600]{2,1,0:T(8,128)(2,1)}) %all-gather.85.cloned.1.call-update) | async-done | bytes 8192016 | tf_op jit(solution)/shard_map/all_gather | solution.py:82
  2090.0 61.2 %reduce-scatter.67.cloned.1.call-done = bf16[32,1280]{1,0:T(8,128)(2,1)} async-done(((bf16[256,1280]{1,0:T(8,128)(2,1)}), bf16[32,1280]{1,0:T(8,128)(2,1)}) %reduce-scatter.67.cloned.1.call-update) | async-done | bytes 81936 | tf_op jit(solution)/shard_map/reduce_scatter | solution.py:493
  2151.3 64.3 %reduce-scatter.65.cloned.1.call-done = bf16[32,1280]{1,0:T(8,128)(2,1)} async-done(((bf16[256,1280]{1,0:T(8,128)(2,1)}), bf16[32,1280]{1,0:T(8,128)(2,1)}) %reduce-scatter.65.cloned.1.call-update) | async-done | bytes 81936 | tf_op jit(solution)/shard_map/reduce_scatter | solution.py:493
  2283.5 67.0 %reduce-scatter.61.cloned.1.call-done = bf16[96,960]{1,0:T(8,128)(2,1)} async-done(((bf16[768,960]{1,0:T(8,128)(2,1)}), bf16[96,960]{1,0:T(8,128)(2,1)}) %reduce-scatter.61.cloned.1.call-update) | async-done | bytes 184336 | tf_op jit(solution)/shard_map/reduce_scatter | solution.py:484
  2352.6 67.7 %reduce-scatter.93.cloned.1.call-done = bf16[320,288]{1,0:T(8,128)(2,1)} async-done(((bf16[2560,288]{1,0:T(8,128)(2,1)}), bf16[320,288]{1,0:T(8,128)(2,1)}) %reduce-scatter.93.cloned.1.call-update) | async-done | bytes 184336
  2422.1 77.4 %reduce-scatter.71.cloned.1.call-done = bf16[640,320]{0,1:T(8,128)(2,1)} async-done(((bf16[640,2560]{0,1:T(8,128)(2,1)}), bf16[640,320]{0,1:T(8,128)(2,1)}) %reduce-scatter.71.cloned.1.call-update) | async-done | bytes 409616 | tf_op jit(solution)/shard_map/reduce_scatter | solution.py:496
  2499.5 79.2 %reduce-scatter.69.cloned.1.call-done = bf16[640,320]{0,1:T(8,128)(2,1)} async-done(((bf16[640,2560]{0,1:T(8,128)(2,1)}), bf16[640,320]{0,1:T(8,128)(2,1)}) %reduce-scatter.69.cloned.1.call-update) | async-done | bytes 409616 | tf_op jit(solution)/shard_map/reduce_scatter | solution.py:496
  2581.1 151.4 %reduce-scatter.83.cloned.1.call-done = bf16[1600,320]{0,1:T(8,128)(2,1)} async-done(((bf16[1600,2560]{0,1:T(8,128)(2,1)}), bf16[1600,320]{0,1:T(8,128)(2,1)}) %reduce-scatter.83.cloned.1.call-update) | async-done | bytes 1024016 | tf_op jit(solution)/shard_map/reduce_scatter | solution.py:508
  2732.5 154.4 %reduce-scatter.81.cloned.1.call-done = bf16[1600,320]{0,1:T(8,128)(2,1)} async-done(((bf16[1600,2560]{0,1:T(8,128)(2,1)}), bf16[1600,320]{0,1:T(8,128)(2,1)}) %reduce-scatter.81.cloned.1.call-update) | async-done | bytes 1024016 | tf_op jit(solution)/shard_map/reduce_scatter | solution.py:508
  2890.8 83.6 %reduce-scatter.59.cloned.1.call-done = bf16[320,768]{1,0:T(8,128)(2,1)} async-done(((bf16[2560,768]{1,0:T(8,128)(2,1)}), bf16[320,768]{1,0:T(8,128)(2,1)}) %reduce-scatter.59.cloned.1.call-update) | async-done | bytes 491536 | tf_op jit(solution)/shard_map/reduce_scatter | solution.py:478
  2974.4 88.6 %reduce-scatter.57.cloned.1.call-done = bf16[320,768]{1,0:T(8,128)(2,1)} async-done(((bf16[2560,768]{1,0:T(8,128)(2,1)}), bf16[320,768]{1,0:T(8,128)(2,1)}) %reduce-scatter.57.cloned.1.call-update) | async-done | bytes 491536 | tf_op jit(solution)/shard_map/reduce_scatter | solution.py:478
  3063.0 154.5 %reduce-scatter.75.cloned.1.call-done = bf16[320,1600]{1,0:T(8,128)(2,1)} async-done(((bf16[2560,1600]{1,0:T(8,128)(2,1)}), bf16[320,1600]{1,0:T(8,128)(2,1)}) %reduce-scatter.75.cloned.1.call-update) | async-done | bytes 1024016 | tf_op jit(solution)/shard_map/reduce_scatter | solution.py:502
  3217.5 154.2 %reduce-scatter.73.cloned.1.call-done = bf16[320,1600]{1,0:T(8,128)(2,1)} async-done(((bf16[2560,1600]{1,0:T(8,128)(2,1)}), bf16[320,1600]{1,0:T(8,128)(2,1)}) %reduce-scatter.73.cloned.1.call-update) | async-done | bytes 1024016 | tf_op jit(solution)/shard_map/reduce_scatter | solution.py:502
  3375.5 150.0 %reduce-scatter.79.cloned.1.call-done = bf16[320,1600]{1,0:T(8,128)(2,1)} async-done(((bf16[2560,1600]{1,0:T(8,128)(2,1)}), bf16[320,1600]{1,0:T(8,128)(2,1)}) %reduce-scatter.79.cloned.1.call-update) | async-done | bytes 1024016 | tf_op jit(solution)/shard_map/reduce_scatter | solution.py:505
  3525.5 154.4 %reduce-scatter.77.cloned.1.call-done = bf16[320,1600]{1,0:T(8,128)(2,1)} async-done(((bf16[2560,1600]{1,0:T(8,128)(2,1)}), bf16[320,1600]{1,0:T(8,128)(2,1)}) %reduce-scatter.77.cloned.1.call-update) | async-done | bytes 1024016 | tf_op jit(solution)/shard_map/reduce_scatter | solution.py:505
  (712 shorter events, 1258.7 us)
Async XLA Ops:
  59.1 282.5 %reduce-scatter.41.cloned.1.call-start = ((), (), s32[]{:S(2)}) async-start(), calls=%async_computation.29 | async-start | bytes 3276800 | tf_op jit(solution)/shard_map/reduce_scatter | solution.py:93
  345.3 281.6 %all-gather.73.cloned.1.call-start = ((), (), s32[]{:S(2)}) async-start(), calls=%async_computation.63 | async-start | bytes 9584640 | tf_op jit(solution)/shard_map/all_gather | solution.py:83
  348.4 406.2 %all-gather.75.cloned.1.call-start = ((), (), s32[]{:S(2)}) async-start(), calls=%async_computation.64 | async-start | bytes 9584640 | tf_op jit(solution)/shard_map/all_gather | solution.py:84
  351.5 446.7 %reduce-scatter.43.cloned.1.call-start = ((), (), s32[]{:S(2)}) async-start(), calls=%async_computation.31 | async-start | bytes 3276800 | tf_op jit(solution)/shard_map/reduce_scatter | solution.py:93
  802.1 278.5 %all-gather.83.cloned.1.call-start = ((), (), s32[]{:S(2)}) async-start(), calls=%async_computation.68 | async-start | bytes 3686400 | tf_op jit(solution)/shard_map/all_gather | solution.py:80
  802.6 317.2 %reduce-scatter.45.cloned.1.call-start = ((), (), s32[]{:S(2)}) async-start(), calls=%async_computation.33 | async-start | bytes 3276800 | tf_op jit(solution)/shard_map/reduce_scatter | solution.py:93
  1089.2 314.5 %all-gather.87.cloned.1.call-start = ((), (), s32[]{:S(2)}) async-start(), calls=%async_computation.70 | async-start | bytes 9584640 | tf_op jit(solution)/shard_map/all_gather | solution.py:83
  1089.8 339.3 %all-gather.53.cloned.1.call-start = ((), (), s32[]{:S(2)}) async-start(), calls=%async_computation.34 | async-start | bytes 3276800 | tf_op jit(solution)/shard_map/all_gather | solution.py:89
  1123.0 435.2 %all-gather.85.cloned.1.call-start = ((), (), s32[]{:S(2)}) async-start(), calls=%async_computation.69 | async-start | bytes 9584640 | tf_op jit(solution)/shard_map/all_gather | solution.py:82
  1123.7 501.7 %reduce-scatter.49.cloned.1.call-start = ((), (), s32[]{:S(2)}) async-start(), calls=%async_computation.37 | async-start | bytes 3276800 | tf_op jit(solution)/shard_map/reduce_scatter | solution.py:331
  1965.8 317.8 %reduce-scatter.63.cloned.1.call-start = ((), (), s32[]{:S(2)}) async-start(), calls=%async_computation.47 | async-start | bytes 1769472 | tf_op jit(solution)/shard_map/reduce_scatter | solution.py:484
  1969.8 380.8 %reduce-scatter.61.cloned.1.call-start = ((), (), s32[]{:S(2)}) async-start(), calls=%async_computation.46 | async-start | bytes 1769472 | tf_op jit(solution)/shard_map/reduce_scatter | solution.py:484
  1973.7 446.5 %reduce-scatter.93.cloned.1.call-start = ((), (), s32[]{:S(2)}) async-start(), calls=%async_computation.76 | async-start | bytes 2211840
  1996.8 502.7 %reduce-scatter.71.cloned.1.call-start = ((), (), s32[]{:S(2)}) async-start(), calls=%async_computation.51 | async-start | bytes 3686400 | tf_op jit(solution)/shard_map/reduce_scatter | solution.py:496
  2002.8 575.9 %reduce-scatter.69.cloned.1.call-start = ((), (), s32[]{:S(2)}) async-start(), calls=%async_computation.50 | async-start | bytes 3686400 | tf_op jit(solution)/shard_map/reduce_scatter | solution.py:496
  2008.8 723.7 %reduce-scatter.83.cloned.1.call-start = ((), (), s32[]{:S(2)}) async-start(), calls=%async_computation.57 | async-start | bytes 9584640 | tf_op jit(solution)/shard_map/reduce_scatter | solution.py:508
  2019.7 867.2 %reduce-scatter.81.cloned.1.call-start = ((), (), s32[]{:S(2)}) async-start(), calls=%async_computation.56 | async-start | bytes 9584640 | tf_op jit(solution)/shard_map/reduce_scatter | solution.py:508
  2030.3 944.1 %reduce-scatter.59.cloned.1.call-start = ((), (), s32[]{:S(2)}) async-start(), calls=%async_computation.45 | async-start | bytes 4423680 | tf_op jit(solution)/shard_map/reduce_scatter | solution.py:478
  2035.4 1027.6 %reduce-scatter.57.cloned.1.call-start = ((), (), s32[]{:S(2)}) async-start(), calls=%async_computation.44 | async-start | bytes 4423680 | tf_op jit(solution)/shard_map/reduce_scatter | solution.py:478
  2043.4 1174.0 %reduce-scatter.75.cloned.1.call-start = ((), (), s32[]{:S(2)}) async-start(), calls=%async_computation.53 | async-start | bytes 9584640 | tf_op jit(solution)/shard_map/reduce_scatter | solution.py:502
  2054.1 1317.6 %reduce-scatter.73.cloned.1.call-start = ((), (), s32[]{:S(2)}) async-start(), calls=%async_computation.52 | async-start | bytes 9584640 | tf_op jit(solution)/shard_map/reduce_scatter | solution.py:502
  2064.7 1460.8 %reduce-scatter.79.cloned.1.call-start = ((), (), s32[]{:S(2)}) async-start(), calls=%async_computation.55 | async-start | bytes 9584640 | tf_op jit(solution)/shard_map/reduce_scatter | solution.py:505
  2075.7 1604.3 %reduce-scatter.77.cloned.1.call-start = ((), (), s32[]{:S(2)}) async-start(), calls=%async_computation.54 | async-start | bytes 9584640 | tf_op jit(solution)/shard_map/reduce_scatter | solution.py:505
  2086.2 1637.0 %all-reduce.22.cloned.1.call-start = ((), (), s32[]{:S(2)}) async-start(), calls=%async_computation.78 | async-start | bytes 2850816 | tf_op jit(solution)/shard_map/psum | solution.py:514
  (202 other events, 7902.6 us)
Sparse Core Ops, SparseCore 0:
  10.8 83.8 all-gather.62
  123.8 70.0 all-gather.64
  344.6 126.6 all-gather.70
  500.2 126.6 all-gather.72
  629.8 124.8 all-gather.74
  800.9 74.4 all-gather.76
  902.9 70.0 all-gather.78
  1149.9 126.6 all-gather.88
  1278.8 124.8 all-gather.86
  1431.5 126.6 all-gather.84
  2019.5 66.6 reduce-scatter.94
  2219.4 64.1 reduce-scatter.62
  2286.8 63.7 reduce-scatter.60
  2354.5 65.7 reduce-scatter.92
  2424.5 74.9 reduce-scatter.70
  2503.5 75.1 reduce-scatter.68
  2582.1 150.3 reduce-scatter.82
  2736.5 150.3 reduce-scatter.80
  2891.0 83.3 reduce-scatter.58
  2978.9 83.9 reduce-scatter.56
  3066.4 150.9 reduce-scatter.74
  3221.3 150.2 reduce-scatter.72
  3375.1 150.3 reduce-scatter.78
  3529.6 150.3 reduce-scatter.76
  (27 shorter events, 892.4 us)
where the time goes:
time: 3740 us; the launch traced here: 3730 us
  waiting for transfers between devices  3060 us (82%)
  matrix products  332 us (9%)
  blocking collectives  148 us (4%)
  local copies, waits for them, and re-layouts  88.8 us (2%)
  other arithmetic  82.9 us (2%)
    reduce_scatter x2, waiting for transfers between devices, body(): lax.psum_scatter(grads[9].astype(jnp.bfloat16), 'dp', scatter_dimension=0...  309 us
    reduce_scatter x2, waiting for transfers between devices, body(): lax.psum_scatter(grads[11].astype(jnp.bfloat16), 'dp', scatter_dimension=...  306 us
    reduce_scatter x2, waiting for transfers between devices, body(): lax.psum_scatter(grads[10].astype(jnp.bfloat16), 'dp', scatter_dimension=...  304 us
    all_gather x2, waiting for transfers between devices, gather_layer(): lax.all_gather(stacks[11][layer_index], 'dp', axis=1, tiled=True)  245 us
    all_gather x2, waiting for transfers between devices, gather_layer(): lax.all_gather(stacks[9][layer_index], 'dp', axis=0, tiled=True)  238 us
    all_gather x2, waiting for transfers between devices, gather_layer(): lax.all_gather(stacks[10][layer_index], 'dp', axis=0, tiled=True)  236 us
    reduce_scatter x2, waiting for transfers between devices, body(): lax.psum_scatter(grads[1].astype(jnp.bfloat16), 'dp', scatter_dimension=0...  172 us
    reduce_scatter x2, waiting for transfers between devices, body(): lax.psum_scatter(grads[7].astype(jnp.bfloat16), 'dp', scatter_dimension=1...  157 us
  transfers between devices with their start and end apart: 51, of which 46 were waited for; matrix products, arithmetic and copies ran while one was open for 9% of the time, Pallas kernels for 0%

commit v1 on v0

v1 whole, which is shorter than its diff:
```python
import functools
import math

import jax
import jax.numpy as jnp
from jax import lax
from jax.sharding import PartitionSpec as P

NOPE = 64
ROPE = 32
VDIM = 64
QR = 768
KVR = 256
LAYERS = 2
QK = 96

epsilon = 1e-05
residual_scale = 1.4 / math.sqrt(62.0)
rope_base = 10000.0
masked_score = -1e30
bf16 = jnp.bfloat16
f32 = jnp.float32

plan = {
    "doc": (0, 3),
    "gains": (0, 1, 2, 3),
    "s": (0, 1, 2),
    "a0": (0, 1, 3),
    "g0": (1, 2, 3, 5, 6),
    "u0": (2, 4, 5, 6, 7),
    "d0": (3, 4, 6, 7, 8),
    "w1": (2, 3, 4, 5),
    "a1": (5, 6, 7, 9),
    "g1": (5, 6, 9, 11, 12),
    "u1": (6, 7, 11, 12, 13),
    "d1": (6, 7, 12, 13, 14),
    "w0": (12, 13, 14, 15),
    "grad d1": (15, 16, 17, 18),
    "grad g1": (16, 17, 18, 19),
    "grad u1": (17, 19, 21, 22),
    "grad a1": (19, 21, 23, 24),
    "grad s1": (21, 22, 23, 24),
    "grad gains1": (20, 21, 22, 23, 24),
    "grad d0": (22, 23, 24, 25),
    "grad g0": (23, 24, 26, 27),
    "grad u0": (24, 26, 27),
    "grad a0": (26, 27),
}

PAIR = 2


def dot(left, right, left_dim, right_dim):
    return lax.dot_general(
        left, right, (((left_dim,), (right_dim,)), ((), ())), preferred_element_type=f32
    )


def norm_parts(values):
    inverse = lax.rsqrt(jnp.mean(values * values, axis=-1, keepdims=True) + epsilon)
    return (values * inverse, inverse)


def norm_back(normed, inverse, gain, upstream):
    scaled = upstream * gain
    result = inverse * (scaled - normed * jnp.mean(scaled * normed, axis=-1, keepdims=True))
    return (result, jnp.sum(upstream * normed, axis=0))


def rotate(rotary, cosine, sine_table):
    half_width = rotary.shape[-1] // 2
    first_half = rotary[..., :half_width]
    second_half = rotary[..., half_width:]
    return jnp.concatenate(
        [
            first_half * cosine - second_half * sine_table,
            second_half * cosine + first_half * sine_table,
        ],
        axis=-1,
    )


def rotate_back(upstream, cosine, sine_table):
    return rotate(upstream, cosine, -sine_table)


class Flow:
    def __init__(self, plan, swap):
        self.plan = plan
        self.swap = swap
        self.count = -1
        self.work = {}
        self.due = {}
        self.results = {}

    def add(self, name, steps):
        self.work[name] = (steps, next(steps), None)
        self.due[name] = list(self.plan.get(name, ()))

    def begin(self, name, steps, request):
        moving = [a if axis is None else self.swap(a, axis, bit) for a, axis, bit in request]
        self.work[name] = (steps, None, moving)

    def advance(self, name, steps, arrived):
        try:
            request = steps.send(arrived)
        except StopIteration as end:
            self.results[name] = end.value
            del self.work[name]
            return
        self.begin(name, steps, request)

    def tick(self, *values):
        self.count += 1
        now = []
        for name in self.work:
            due = self.due[name]
            if due and due[0] <= self.count:
                due.pop(0)
                now.append(name)
        held = []
        for name in now:
            _, request, moving = self.work[name]
            held.append([a for a, _, _ in request] if moving is None else moving)
        flat = [a for arrays in held for a in arrays]
        values = list(values)
        if flat:
            out = lax.optimization_barrier((*values, *flat))
            values, flat = list(out[: len(values)]), list(out[len(values) :])
        for name, arrays in zip(now, held):
            tied, flat = flat[: len(arrays)], flat[len(arrays) :]
            steps, request, moving = self.work[name]
            if moving is None:
                self.begin(name, steps, [(a, *r[1:]) for a, r in zip(tied, request)])
            else:
                self.advance(name, steps, tied)
        return values[0] if len(values) == 1 else values

    def result(self, name):
        while name in self.work:
            steps, request, moving = self.work[name]
            if moving is None:
                self.begin(name, steps, request)
            else:
                self.advance(name, steps, moving)
        return self.results[name]


class Place:
    def __init__(self, dp, tensor):
        self.flow = Flow(plan, self.swap)
        self.dp = dp
        self.tensor = tensor
        self.group_bits = [1 << j for j in reversed(range(dp.bit_length() - 1)) if 1 << j != PAIR]
        self.pieces = dp // 2
        self.here = lax.axis_index("dp")
        self.column = lax.axis_index("tensor")
        self.low = (self.here & PAIR) == 0
        self.pairs = [
            [(base | pair * PAIR) * tensor + t for pair in range(2) for t in range(tensor)]
            for base in range(dp)
            if not base & PAIR
        ]

    def swap(self, array, axis, bit):
        size = self.dp if axis == "dp" else self.tensor
        return lax.ppermute(array, axis, [(i, i ^ bit) for i in range(size)])

    def relative(self, piece):
        return sum(bit for j, bit in enumerate(self.group_bits) if piece >> j & 1)

    def order(self):
        return [
            (self.relative(piece) | pair * PAIR)
            for piece in range(self.pieces)
            for pair in range(2)
        ]

    def flip(self, blocks):
        for bit in self.group_bits:
            own = (self.here & bit) != 0
            blocks = [jnp.where(own, blocks[k ^ bit], blocks[k]) for k in range(self.dp)]
        return blocks

    def to_group(self, array, axis):
        blocks = self.flip(jnp.split(array, self.dp, axis=axis))
        return jnp.concatenate([blocks[k] for k in self.order()], axis=axis)

    def from_group(self, array, axis):
        parts = jnp.split(array, self.dp, axis=axis)
        blocks = [None] * self.dp
        for part, k in zip(parts, self.order()):
            blocks[k] = part
        return jnp.concatenate(self.flip(blocks), axis=axis)

    def gather_all(self, array):
        blocks = array[None]
        for j in range(self.dp.bit_length() - 1):
            (taken,) = yield [(blocks, "dp", 1 << j)]
            blocks = jnp.concatenate([blocks, taken], axis=0)
        blocks = [blocks[k] for k in range(self.dp)]
        for j in range(self.dp.bit_length() - 1):
            own = (self.here & (1 << j)) != 0
            blocks = [jnp.where(own, blocks[k ^ (1 << j)], blocks[k]) for k in range(self.dp)]
        return jnp.stack(blocks)

    def gather_weight(self, prepare, *arrays):
        if arrays:
            arrays = yield [(a, None, 0) for a in arrays]
        low, high = prepare(*arrays)
        mine = jnp.where(self.low, low, high)
        (taken,) = yield [(jnp.where(self.low, high, low), "dp", PAIR)]
        pieces = [
            jnp.concatenate(
                [jnp.where(self.low, mine, taken), jnp.where(self.low, taken, mine)], axis=0
            )
        ]
        pieces = yield from self.gather_pieces(pieces)
        return jnp.concatenate(pieces, axis=0)

    def gather_pieces(self, pieces):
        total = len(self.group_bits)
        held = {0: pieces[0]}
        for moves in range(1, total + 1):
            wanted = [k for k in range(1 << total) if k.bit_count() == moves]
            taken = yield [
                (held[k & ~(1 << j)], "dp", self.group_bits[j])
                for k in wanted
                for j in [k.bit_length() - 1]
            ]
            held.update(zip(wanted, taken))
        return [held[k] for k in range(1 << total)]

    def scatter_grad(self, prepare, *arrays):
        if arrays:
            arrays = yield [(a, None, 0) for a in arrays]
        send, keep = prepare(*arrays)
        for bit in reversed(self.group_bits):
            (taken,) = yield [(send, "dp", bit)]
            total = (keep.astype(f32) + taken.astype(f32)).astype(bf16)
            keep, send = jnp.split(total, 2, axis=0)
        (taken,) = yield [(jnp.where(self.low, send, keep), "dp", PAIR)]
        mine = jnp.where(self.low, keep, send)
        return jnp.where(self.low, mine, taken), jnp.where(self.low, taken, mine)

    def gather_whole(self, share):
        (share,) = yield [(share, None, 0)]
        pieces = yield from self.gather_pieces([share])
        joined = self.gather_rows(jnp.concatenate(pieces, axis=0), tiled=False)
        rows, columns = share.shape
        joined = joined.reshape(2, self.tensor, self.pieces, rows, columns)
        return joined.transpose(2, 0, 1, 3, 4).reshape(-1, columns)

    def sum_all(self, blocks):
        blocks = [blocks[k] for k in range(self.dp)]
        bits = [1 << j for j in range(self.dp.bit_length() - 1)]
        for bit in bits:
            own = (self.here & bit) != 0
            blocks = [jnp.where(own, blocks[k ^ bit], blocks[k]) for k in range(self.dp)]
        total = jnp.stack(blocks)
        for bit in reversed(bits):
            half = total.shape[0] // 2
            (taken,) = yield [(total[half:], "dp", bit)]
            total = total[:half] + taken
        for bit in (1, 2):
            (taken,) = yield [(total, "tensor", bit)]
            total = total + taken
        return total[0]

    def gather_rows(self, rows, tiled=True):
        return lax.all_gather(
            rows, ("dp", "tensor"), axis=0, tiled=tiled, axis_index_groups=self.pairs
        )

    def relative_rows(self, rows):
        count = rows.shape[0] // (2 * self.tensor)
        own = jnp.where(self.low, 0, self.tensor) + self.column

        def half(core):
            return jnp.concatenate(
                [
                    lax.dynamic_slice_in_dim(
                        rows, (own ^ (pair * self.tensor + across * 2 + core)) * count, count, 0
                    )
                    for pair in range(2)
                    for across in range(2)
                ],
                axis=0,
            )

        return half(0), half(1)

    def scatter_rows(self, own, other):
        count = own.shape[0] // 4
        half = count // 2
        taken = self.swap(other, "tensor", 1)
        total = (own.astype(f32) + taken.astype(f32)).astype(bf16)
        rows, across, along = total[:count], total[count : 2 * count], total[2 * count : 3 * count]
        corner_first = self.swap(total[3 * count : 3 * count + half], "dp", PAIR)
        corner_second = self.swap(total[3 * count + half :], "tensor", 2)
        across = jnp.concatenate(
            [(across[:half].astype(f32) + corner_first.astype(f32)).astype(bf16), across[half:]],
            axis=0,
        )
        along = jnp.concatenate(
            [along[:half], (along[half:].astype(f32) + corner_second.astype(f32)).astype(bf16)],
            axis=0,
        )
        across = self.swap(across, "tensor", 2)
        along = self.swap(along, "dp", PAIR)
        return rows.astype(f32) + across.astype(f32) + along.astype(f32)

    def own_rows(self, rows):
        count = rows.shape[0] // (2 * self.tensor)
        own = jnp.where(self.low, 0, self.tensor) + self.column
        return lax.dynamic_slice_in_dim(rows, own * count, count, 0)

    def in_order(self, array, axis, bit, place_axis):
        taken = self.swap(array, axis, bit)
        index = self.here if axis == "dp" else self.column
        first = (index & bit) == 0
        return jnp.stack(
            [jnp.where(first, array, taken), jnp.where(first, taken, array)], axis=place_axis
        )


def tables(docs):
    rows_total = docs.shape[1]
    spots = jnp.arange(rows_total, dtype=jnp.int32)
    same = docs[:, :, None] == docs[:, None, :]
    allowed = same & (spots[:, None] >= spots[None, :])
    starts = jnp.sum((docs[:, None, :] < docs[:, :, None]).astype(jnp.int32), axis=-1)
    positions = (spots[None, :] - starts).astype(f32)
    frequency = rope_base ** (-jnp.arange(0, ROPE, 2, dtype=f32) / ROPE)
    angles = positions[..., None] * frequency
    return (jnp.cos(angles), jnp.sin(angles), allowed)


def scores_of(queries, key_rows, allowed):
    scores = jnp.einsum("bqhd,bkhd->bhqk", queries, key_rows, preferred_element_type=f32)
    return jnp.where(allowed[:, None], scores * (1.0 / math.sqrt(QK)), masked_score)


def attend_forward(queries, key_rows, values, allowed):
    scores = scores_of(queries, key_rows, allowed)
    highest = jnp.max(scores, axis=-1, keepdims=True)
    expanded = jnp.exp(scores - highest)
    totals = jnp.sum(expanded, axis=-1, keepdims=True)
    probs_low = (expanded / totals).astype(bf16)
    attended = jnp.einsum("bhqk,bkhd->bqhd", probs_low, values, preferred_element_type=f32)
    return (attended, highest + jnp.log(totals))


def attend_backward(queries, key_rows, values, allowed, log_totals, att_grad):
    scale_factor = 1.0 / math.sqrt(QK)
    probability = jnp.exp(scores_of(queries, key_rows, allowed) - log_totals)
    probs_low = probability.astype(bf16)
    value_grad = jnp.einsum("bhqk,bqhd->bkhd", probs_low, att_grad, preferred_element_type=f32)
    prob_grad = jnp.einsum("bqhd,bkhd->bhqk", att_grad, values, preferred_element_type=f32)
    inner_sum = jnp.sum(prob_grad * probability, axis=-1, keepdims=True)
    score_grad = (probability * (prob_grad - inner_sum)).astype(bf16)
    query_grad = (
        jnp.einsum("bhqk,bkhd->bqhd", score_grad, key_rows, preferred_element_type=f32)
        * scale_factor
    )
    key_grad = (
        jnp.einsum("bhqk,bqhd->bkhd", score_grad, queries, preferred_element_type=f32)
        * scale_factor
    )
    return query_grad, key_grad, value_grad


def rotate_own(place, array, cosine, sine_table):
    flat = (-1, cosine.shape[-1])
    return rotate(
        array, place.own_rows(cosine.reshape(flat)), place.own_rows(sine_table.reshape(flat))
    )


def first_latents(place, shares, cosine, sine_table, gains):
    _, _, q_gain, kv_gain, _ = gains
    width = QR // shares.shape[0]
    rows_total = shares.shape[1]
    q_latent = jnp.swapaxes(shares[..., :width], 0, 1).reshape(rows_total, -1).astype(f32)
    kv_latent = jnp.swapaxes(shares[..., width:], 0, 1).reshape(rows_total, -1).astype(f32)
    q_normed, q_inverse = norm_parts(q_latent)
    kv_normed, kv_inverse = norm_parts(kv_latent[:, :KVR])
    flat = (-1, cosine.shape[-1])
    shared = rotate(kv_latent[:, KVR:], cosine.reshape(flat), sine_table.reshape(flat))
    latents = jnp.concatenate([q_normed * q_gain, kv_normed * kv_gain, shared], axis=1)
    own = [place.own_rows(v) for v in (q_normed, q_inverse, kv_normed, kv_inverse)]
    return latents.astype(bf16), own


def own_latents(place, low_in, down_latent, cosine, sine_table, gains):
    _, _, q_gain, kv_gain, _ = gains
    latent = dot(low_in, down_latent, 1, 0)
    q_normed, q_inverse = norm_parts(latent[:, :QR])
    kv_normed, kv_inverse = norm_parts(latent[:, QR : QR + KVR])
    shared = rotate_own(place, latent[:, QR + KVR :], cosine, sine_table)
    packed = jnp.concatenate([q_normed * q_gain, kv_normed * kv_gain, shared], axis=1).astype(bf16)
    return packed, [q_normed, q_inverse, kv_normed, kv_inverse]


def layer_forward(place, layer, rows_in, latents, cosine, sine_table, allowed, gains):
    flow = place.flow
    gain_post = gains[4]
    group_rows = allowed.shape[1]
    q_up, kv_up, out_t = flow.result(f"a{layer}")
    latents, q_up, kv_up, out_t = flow.tick(latents, q_up, kv_up, out_t)
    heads = q_up.shape[1] // QK
    q_low = latents[:, :QR]
    kv_low = latents[:, QR : QR + KVR]
    q_full = dot(q_low, q_up, 1, 0).reshape(2, group_rows, heads, QK)
    kv_full = dot(kv_low, kv_up, 1, 0).reshape(2, group_rows, heads, NOPE + VDIM)
    queries = jnp.concatenate(
        [
            q_full[..., :NOPE],
            rotate(q_full[..., NOPE:], cosine[:, :, None, :], sine_table[:, :, None, :]),
        ],
        axis=-1,
    ).astype(bf16)
    key_rows = jnp.concatenate(
        [
            kv_full[..., :NOPE].astype(bf16),
            jnp.broadcast_to(
                latents[:, QR + KVR :].reshape(2, group_rows, 1, ROPE),
                (2, group_rows, heads, ROPE),
            ),
        ],
        axis=-1,
    )
    values = kv_full[..., NOPE:].astype(bf16)
    attended, log_totals = attend_forward(queries, key_rows, values, allowed)
    att_low = attended.reshape(2 * group_rows, heads * VDIM).astype(bf16)
    att_low = flow.tick(att_low)
    att_own, att_other = place.relative_rows(att_low)
    middle = rows_in + residual_scale * place.scatter_rows(
        dot(att_own, out_t, 1, 1).astype(bf16), dot(att_other, out_t, 1, 1).astype(bf16)
    )
    middle = flow.tick(middle)
    normed_mid, inv_mid = norm_parts(middle)
    all_mid = place.gather_rows((normed_mid * gain_post).astype(bf16))
    all_mid = flow.tick(all_mid)
    gate = flow.result(f"g{layer}")
    up = flow.result(f"u{layer}")
    gate_act = dot(all_mid, gate, 1, 0)
    up_act = dot(all_mid, up, 1, 0)
    hidden = (jax.nn.silu(gate_act) * up_act).astype(bf16)
    hidden = flow.tick(hidden)
    down_t = flow.result(f"d{layer}")
    hidden_own, hidden_other = place.relative_rows(hidden)
    result = middle + residual_scale * place.scatter_rows(
        dot(hidden_own, down_t, 1, 1).astype(bf16), dot(hidden_other, down_t, 1, 1).astype(bf16)
    )
    stored = (
        q_low,
        kv_low,
        queries,
        key_rows,
        values,
        log_totals,
        att_low,
        normed_mid,
        inv_mid,
        all_mid,
        gate_act,
        up_act,
        hidden,
    )
    return (result, stored, (q_up, kv_up, out_t, gate, up, down_t))


def layer_backward(
    place, layer, grad_rows, branch_two, weights, before, stored, cosine, sine_table, allowed, gains
):
    q_up, kv_up, out_t, gate, up, down_t = weights
    gain_in, _, q_gain, kv_gain, gain_post = gains
    normed_in, inv_in, all_in, q_normed, q_inverse, kv_normed, kv_inverse = before
    (
        q_low,
        kv_low,
        queries,
        key_rows,
        values,
        log_totals,
        att_low,
        normed_mid,
        inv_mid,
        all_mid,
        gate_act,
        up_act,
        hidden,
    ) = stored
    group_rows = allowed.shape[1]
    heads = q_up.shape[1] // QK
    flow = place.flow

    def in_halves(left, right):
        half = left.shape[1] // 2
        return (
            dot(left[:, half:], right, 0, 0).astype(bf16),
            dot(left[:, :half], right, 0, 0).astype(bf16),
        )

    flow.add(f"grad d{layer}", place.scatter_grad(lambda: in_halves(branch_two, hidden)))
    grad_hidden = dot(branch_two, down_t, 1, 0)
    logistic = jax.nn.sigmoid(gate_act)
    gate_low = (
        grad_hidden * up_act * logistic * (1.0 + gate_act * (1.0 - logistic))
    ).astype(bf16)
    up_low = (grad_hidden * gate_act * logistic).astype(bf16)
    gate_low, up_low = flow.tick(gate_low, up_low)
    gate_own, gate_other = place.relative_rows(gate_low)
    up_own, up_other = place.relative_rows(up_low)
    mid_grad = place.scatter_rows(
        (dot(gate_own, gate, 1, 1) + dot(up_own, up, 1, 1)).astype(bf16),
        (dot(gate_other, gate, 1, 1) + dot(up_other, up, 1, 1)).astype(bf16),
    )
    flow.add(f"grad g{layer}", place.scatter_grad(lambda: in_halves(all_mid, gate_low)))
    flow.add(f"grad u{layer}", place.scatter_grad(lambda: in_halves(all_mid, up_low)))
    mid_grad = flow.tick(mid_grad)
    back_mid, grad_gain_post = norm_back(normed_mid, inv_mid, gain_post, mid_grad)
    grad_middle = grad_rows + back_mid
    branch_one = place.gather_rows((residual_scale * grad_middle).astype(bf16))
    branch_one = flow.tick(branch_one)
    att_grad = dot(branch_one, out_t, 1, 0).astype(bf16).reshape(2, group_rows, heads, VDIM)
    query_grad, key_grad, value_grad = attend_backward(
        queries, key_rows, values, allowed, log_totals, att_grad
    )
    q_full_grad = (
        jnp.concatenate(
            [
                query_grad[..., :NOPE],
                rotate_back(
                    query_grad[..., NOPE:], cosine[:, :, None, :], sine_table[:, :, None, :]
                ),
            ],
            axis=-1,
        )
        .astype(bf16)
        .reshape(2 * group_rows, heads * QK)
    )
    shared_grad = rotate_back(jnp.sum(key_grad[..., NOPE:], axis=2), cosine, sine_table)
    kv_full_grad = (
        jnp.concatenate([key_grad[..., :NOPE], value_grad], axis=-1)
        .astype(bf16)
        .reshape(2 * group_rows, heads * (NOPE + VDIM))
    )
    latent_part = jnp.concatenate(
        [
            dot(q_full_grad, q_up, 1, 1),
            dot(kv_full_grad, kv_up, 1, 1),
            shared_grad.reshape(2 * group_rows, ROPE),
        ],
        axis=1,
    ).astype(bf16)
    latent_part = flow.tick(latent_part)
    latent_grad = place.scatter_rows(*place.relative_rows(latent_part))

    def attention_grads():
        (pack,) = pack_attention(
            [place.to_group(dot(q_low, q_full_grad, 0, 0).astype(bf16), 0)],
            [place.to_group(dot(kv_low, kv_full_grad, 0, 0).astype(bf16), 0)],
            [dot(branch_one, att_low, 0, 0).astype(bf16)],
            place.dp,
        )
        keep, send = jnp.split(pack, 2, axis=0)
        return send, keep

    flow.add(f"grad a{layer}", place.scatter_grad(attention_grads))
    latent_grad = flow.tick(latent_grad)
    down_latent = flow.result(f"w{layer}")
    q_latent_grad, grad_q_gain = norm_back(q_normed, q_inverse, q_gain, latent_grad[:, :QR])
    kv_part_grad, grad_kv_gain = norm_back(
        kv_normed, kv_inverse, kv_gain, latent_grad[:, QR : QR + KVR]
    )
    latent_low = jnp.concatenate(
        [q_latent_grad, kv_part_grad, latent_grad[:, QR + KVR :]], axis=1
    ).astype(bf16)
    in_grad = dot(latent_low, down_latent, 1, 1)
    back_in, grad_gain_in = norm_back(normed_in, inv_in, gain_in, in_grad)
    grad_rows = flow.tick(grad_middle + back_in)
    next_branch = None
    if layer:
        next_branch = place.gather_rows((residual_scale * grad_rows).astype(bf16))
    latent_all = place.gather_rows(latent_low)
    q_width = QR // (2 * place.tensor)
    kv_width = (KVR + ROPE) // (2 * place.tensor)
    share = jnp.where(place.low, 0, place.tensor) + place.column

    def share_grads():
        latent_share = jnp.concatenate(
            [
                lax.dynamic_slice_in_dim(latent_all[:, :QR], share * q_width, q_width, 1),
                lax.dynamic_slice_in_dim(latent_all[:, QR:], share * kv_width, kv_width, 1),
            ],
            axis=1,
        )
        return in_halves(all_in, latent_share)

    def share_steps():
        low, high = yield from place.scatter_grad(share_grads)
        joined = jnp.stack([low, high])
        for bit in (1, 2):
            (taken,) = yield [(joined, "tensor", bit)]
            first = (place.column & bit) == 0
            joined = jnp.stack(
                [jnp.where(first, joined, taken), jnp.where(first, taken, joined)], axis=1
            )
        joined = joined.reshape(2 * place.tensor, *joined.shape[-2:]).swapaxes(0, 1)
        rows = joined.shape[0]
        return joined[..., :q_width].reshape(rows, -1), joined[..., q_width:].reshape(rows, -1)

    flow.add(f"grad s{layer}", share_steps())
    dp = place.dp
    flow.add(
        f"grad gains{layer}",
        place.sum_all(
            jnp.concatenate(
                [
                    place.from_group(grad_gain_in, 0).reshape(dp, -1),
                    grad_q_gain.reshape(dp, -1),
                    grad_kv_gain.reshape(dp, -1),
                    place.from_group(grad_gain_post, 0).reshape(dp, -1),
                ],
                axis=1,
            )
        ),
    )
    return (grad_rows, next_branch)


def pack_attention(q_ups, kv_ups, outs, blocks):
    packs = []
    for q_up, kv_up, out in zip(q_ups, kv_ups, outs):
        columns = kv_up.shape[-1]
        q_up = q_up.reshape(blocks, -1, q_up.shape[-1])
        q_up = jnp.pad(q_up, ((0, 0), (0, 0), (0, columns - q_up.shape[-1])))
        out = out.reshape(blocks, -1, out.shape[-1])
        half = out.shape[1] // 2
        out = jnp.concatenate([out[:, :half], out[:, half:]], axis=2)
        packs.append(
            jnp.concatenate([q_up, kv_up.reshape(blocks, -1, columns), out], axis=1).reshape(
                -1, columns
            )
        )
    return packs


def unpack_attention(pack, blocks, q_rows, kv_rows):
    columns = pack.shape[-1]
    heads = columns // (NOPE + VDIM)
    pack = pack.reshape(blocks, -1, columns)
    q_up = pack[:, :q_rows, : heads * QK].reshape(blocks * q_rows, -1)
    kv_up = pack[:, q_rows : q_rows + kv_rows].reshape(blocks * kv_rows, -1)
    out = pack[:, q_rows + kv_rows :]
    width = heads * VDIM
    out = jnp.concatenate([out[..., :width], out[..., width:]], axis=1).reshape(-1, width)
    return q_up, kv_up, out


def body(
    sizes,
    layer_input,
    doc_ids,
    norm_in,
    q_down,
    q_gain,
    q_up,
    kv_down,
    kv_gain,
    kv_up,
    out_proj,
    norm_post,
    gate_proj,
    up_proj,
    down_proj,
    out_grad,
):
    place = Place(*sizes)
    flow = place.flow
    dp = place.dp

    def halves(array):
        return jnp.split(array, 2, axis=-1)

    q_width = QR // (2 * place.tensor)
    kv_width = (KVR + ROPE) // (2 * place.tensor)

    def share_of(pair):
        share = pair * place.tensor + place.column
        joined = jnp.concatenate(
            [
                lax.dynamic_slice_in_dim(q_down[0], share * q_width, q_width, 1),
                lax.dynamic_slice_in_dim(kv_down[0], share * kv_width, kv_width, 1),
            ],
            axis=1,
        )
        return (joined.astype(f32) * norm_in[0].astype(f32)[:, None]).astype(bf16)

    def doc_steps():
        (taken,) = yield [(doc_ids, "dp", PAIR)]
        return jnp.stack(
            [jnp.where(place.low, doc_ids, taken), jnp.where(place.low, taken, doc_ids)]
        )

    def attention_halves(layer_q_up, layer_kv_up, layer_out):
        return [
            pack_attention(
                [halves(layer_q_up)[pair]], [halves(layer_kv_up)[pair]], [halves(layer_out.T)[pair]], 1
            )[0]
            for pair in range(2)
        ]

    def attention_steps(layer):
        arrays = (q_up[layer], kv_up[layer], out_proj[layer])
        if layer:
            pack = yield from place.gather_weight(attention_halves, *arrays)
        else:
            pack = yield from place.gather_weight(lambda: attention_halves(*arrays))
        layer_q_up, layer_kv_up, layer_out = unpack_attention(
            pack, dp, q_up.shape[1], kv_up.shape[1]
        )
        return place.from_group(layer_q_up, 0), place.from_group(layer_kv_up, 0), layer_out

    flow.add("s", place.gather_weight(lambda: (share_of(0), share_of(1))))
    flow.add("doc", doc_steps())
    flow.add(
        "gains", place.gather_all(jnp.concatenate([norm_in, q_gain, kv_gain, norm_post], axis=1))
    )
    share_rows = q_down.shape[1] // place.tensor
    for layer in range(LAYERS):
        flow.add(f"a{layer}", attention_steps(layer))
        flow.add(f"g{layer}", place.gather_weight(halves, gate_proj[layer]))
        flow.add(f"u{layer}", place.gather_weight(halves, up_proj[layer]))
        flow.add(f"d{layer}", place.gather_weight(lambda a: halves(a.T), down_proj[layer]))
        flow.add(
            f"w{layer}",
            place.gather_whole(
                lax.dynamic_slice_in_dim(
                    jnp.concatenate([q_down[layer], kv_down[layer]], axis=1),
                    place.column * share_rows,
                    share_rows,
                    0,
                )
            ),
        )

    current = place.to_group(layer_input, 1).astype(f32)
    grad_rows = place.to_group(out_grad, 1).astype(f32)
    before = []
    stored = []
    weights = []
    current = flow.tick(current)
    normed_in, inv_in = norm_parts(current)
    all_in = place.gather_rows(normed_in.astype(bf16))
    current = flow.tick(current)
    current = flow.tick(current)
    share = flow.tick(dot(all_in, flow.result("s"), 1, 0).astype(bf16))
    cosine, sine_table, allowed = tables(flow.result("doc"))
    gathered_gains = flow.result("gains").astype(f32)
    widths = [norm_in.shape[1], q_gain.shape[1], kv_gain.shape[1], norm_post.shape[1]]
    starts = [sum(widths[:k]) for k in range(5)]

    def gain_of(layer, position):
        return gathered_gains[:, layer, starts[position] : starts[position + 1]].reshape(-1)

    gains = [
        (
            place.to_group(gain_of(layer, 0), 0),
            None,
            gain_of(layer, 1),
            gain_of(layer, 2),
            place.to_group(gain_of(layer, 3), 0),
        )
        for layer in range(LAYERS)
    ]
    branch = None
    for layer in range(LAYERS):
        if layer == 0:
            latents, kept = first_latents(
                place, place.gather_rows(share, tiled=False), cosine, sine_table, gains[layer]
            )
        else:
            normed_in, inv_in = norm_parts(current)
            low_in = (normed_in * gains[layer][0]).astype(bf16)
            packed, kept = own_latents(
                place, low_in, flow.result(f"w{layer}"), cosine, sine_table, gains[layer]
            )
            packed, low_in = flow.tick(packed, low_in)
            latents = place.gather_rows(packed)
            all_in = place.gather_rows(low_in)
        before.append((normed_in, inv_in, all_in, *kept))
        current, kept, layer_weights = layer_forward(
            place, layer, current, latents, cosine, sine_table, allowed, gains[layer]
        )
        stored.append(kept)
        weights.append(layer_weights)
    branch = place.gather_rows((residual_scale * grad_rows).astype(bf16))
    for layer in reversed(range(LAYERS)):
        if layer < LAYERS - 1:
            branch = flow.tick(branch)
        grad_rows, branch = layer_backward(
            place,
            layer,
            grad_rows,
            branch,
            weights[layer],
            before[layer],
            stored[layer],
            cosine,
            sine_table,
            allowed,
            gains[layer],
        )
    layer_grads = []
    for layer in range(LAYERS):
        grad_q_down, grad_kv_down = (a.astype(f32) for a in flow.result(f"grad s{layer}"))
        if layer == 0:
            scale = norm_in[0].astype(f32)[:, None]
            grad_q_down = grad_q_down * scale
            grad_kv_down = grad_kv_down * scale
        attention_low, attention_high = (
            unpack_attention(a, 1, q_up.shape[1], kv_up.shape[1])
            for a in flow.result(f"grad a{layer}")
        )
        gain_grads = flow.result(f"grad gains{layer}")

        def joined(low, high):
            return jnp.concatenate([low, high], axis=1).astype(f32)

        layer_grads.append(
            (
                grad_q_down,
                joined(attention_low[0], attention_high[0]),
                grad_kv_down,
                joined(attention_low[1], attention_high[1]),
                joined(attention_low[2], attention_high[2]).T,
                joined(*flow.result(f"grad g{layer}")),
                joined(*flow.result(f"grad u{layer}")),
                joined(*flow.result(f"grad d{layer}")).T,
                *[gain_grads[starts[k] : starts[k + 1]] for k in range(4)],
            )
        )
    stacked = [jnp.stack([grads[position] for grads in layer_grads]) for position in range(12)]
    return (
        place.from_group(current.astype(bf16), 1),
        place.from_group(grad_rows.astype(bf16), 1),
        stacked[8],
        stacked[0],
        stacked[9],
        stacked[1],
        stacked[2],
        stacked[10],
        stacked[3],
        stacked[4],
        stacked[11],
        stacked[5],
        stacked[6],
        stacked[7],
    )


def solution(mesh):
    in_specs = (
        P(("dp", "tensor"), None),
        P("dp"),
        P(None, "dp"),
        P(None, "dp", None),
        P(None, "dp"),
        P(None, "dp", "tensor"),
        P(None, "dp", None),
        P(None, "dp"),
        P(None, "dp", "tensor"),
        P(None, "tensor", "dp"),
        P(None, "dp"),
        P(None, "dp", "tensor"),
        P(None, "dp", "tensor"),
        P(None, "tensor", "dp"),
        P(("dp", "tensor"), None),
    )
    out_specs = (
        P(("dp", "tensor"), None),
        P(("dp", "tensor"), None),
        P(None, "dp"),
        P(None, "dp", None),
        P(None, "dp"),
        P(None, "dp", "tensor"),
        P(None, "dp", None),
        P(None, "dp"),
        P(None, "dp", "tensor"),
        P(None, "tensor", "dp"),
        P(None, "dp"),
        P(None, "dp", "tensor"),
        P(None, "dp", "tensor"),
        P(None, "tensor", "dp"),
    )
    sizes = (mesh.shape["dp"], mesh.shape["tensor"])
    return jax.shard_map(
        functools.partial(body, sizes),
        mesh=mesh,
        in_specs=in_specs,
        out_specs=out_specs,
        check_vma=False,
    )
```

time: 3740 us -> 1650 us (0.44)
  waiting for transfers between devices: 3060 us -> 685 us
  local copies, waits for them, and re-layouts: 88.8 us -> 310 us
  blocking collectives: 148 us -> 0 us
  starting transfers between devices: 5.29 us -> 139 us
  other arithmetic: 82.9 us -> 213 us
  matrix products: 332 us -> 274 us
    reduce_scatter x22 -> x0, waiting for transfers between devices: 1660 us -> none  [the longest x2 309 us: body(): lax.psum_scatter(grads[9].astype(jnp.bfloat16), 'dp', scatter_dimension=0...]
    all_gather x22 -> x14, waiting for transfers between devices: 1250 us -> 38.5 us  [gather_rows(): lax.all_gather(rows, ('dp', 'tensor'), axis=0, tiled=tiled, axis_index_gr...]
    ppermute x0 -> x130, waiting for transfers between devices: none -> 646 us  [swap(): return lax.ppermute(array, axis, [(i, i ^ bit) for i in range(size)])]
    ppermute x0 -> x130, starting transfers between devices: none -> 137 us  [swap(): return lax.ppermute(array, axis, [(i, i ^ bit) for i in range(size)])]
    unnamed x57 -> x14, waiting for transfers between devices: 104 us -> 0.75 us
    unnamed x2 -> x0, blocking collectives: 75.8 us -> none
    all_gather x2 -> x0, blocking collectives: 66.9 us -> none  [gather_layer(): lax.all_gather(stacks[6][layer_index], 'dp', axis=0, tiled=True)]
    concatenate x0 -> x29, local copies, waits for them, and re-layouts: none -> 66.2 us  [the longest x9 48.8 us: gather_weight(): return jnp.concatenate(pieces, axis=0)]
  transfers between devices with their start and end apart: 51 -> 144, of which waited for: 46 -> 63; matrix products, arithmetic and copies ran while one was open for 9% -> 36% of each run, Pallas kernels for 0% -> 0%
where the time goes in v1:
time: 1650 us; the launch traced here: 1640 us
  waiting for transfers between devices  685 us (42%)
  local copies, waits for them, and re-layouts  310 us (19%)
  matrix products  274 us (17%)
  other arithmetic  213 us (13%)
  starting transfers between devices  139 us (8%)
  between operations  20.2 us (1%)
    ppermute x130, waiting for transfers between devices, swap(): return lax.ppermute(array, axis, [(i, i ^ bit) for i in range(size)])  646 us
    dot_general x58, matrix products, dot(): lax.dot_general(left, right, (((left_dim,), (right_dim,)), ((), ())), pre...  232 us
    ppermute x130, starting transfers between devices, swap(): return lax.ppermute(array, axis, [(i, i ^ bit) for i in range(size)])  137 us
    unnamed x772, local copies, waits for them, and re-layouts  99.5 us
    concatenate x9, local copies, waits for them, and re-layouts, gather_weight(): return jnp.concatenate(pieces, axis=0)  48.8 us
    all_gather x14, waiting for transfers between devices, gather_rows(): lax.all_gather(rows, ('dp', 'tensor'), axis=0, tiled=tiled, axis_index_gr...  38.5 us
  transfers between devices with their start and end apart: 144, of which 63 were waited for; matrix products, arithmetic and copies ran while one was open for 36% of the time, Pallas kernels for 0%

profile of v1, /device:TPU:0, one launch (start us, length us, event | category | flops | bytes accessed | tf_op | source)
XLA Modules:
  0.0 1640.4 jit_solution(18231111640767524469)
XLA Ops:
  63.6 13.1 collective-permute-done.6
  108.1 29.0 %collective-permute-done.12 = bf16[576,640]{1,0:T(8,128)(2,1)S(1)} collective-permute-done((bf16[576,640]{1,0:T(8,128)(2,1)}, bf16[576,640]{1,0:T(8,128)(2,1)S(1)}, u32[]{:S(2)}, u32[]{:S(2)}) %collective-permute-start.12) | collective-permute-done | bytes 737312 | tf_op jit(solution)/shard_map/ppermute | solution.py:167
  252.9 13.8 collective-permute-done.23
  268.5 22.5 %collective-permute-done.27 = bf16[320,800]{1,0:T(8,128)(2,1)S(1)} collective-permute-done((bf16[320,800]{1,0:T(8,128)(2,1)}, bf16[320,800]{1,0:T(8,128)(2,1)S(1)}, u32[]{:S(2)}, u32[]{:S(2)}) %collective-permute-start.27) | collective-permute-done | bytes 512032 | tf_op jit(solution)/shard_map/ppermute | solution.py:167
  317.3 29.0 %collective-permute-done.31 = bf16[288,640]{1,0:T(8,128)(2,1)} collective-permute-done((bf16[288,640]{1,0:T(8,128)(2,1)}, bf16[288,640]{1,0:T(8,128)(2,1)}, u32[]{:S(2)}, u32[]{:S(2)}) %collective-permute-start.31) | collective-permute-done | bytes 368672 | tf_op jit(solution)/shard_map/ppermute | solution.py:167
  346.3 11.0 all-gather.20.cloned.1.call-done
  501.3 12.2 all-gather.22.cloned.1.call-done
  585.8 14.7 collective-permute-done.49
  603.1 20.3 %collective-permute-done.53 = bf16[320,800]{1,0:T(8,128)(2,1)S(1)} collective-permute-done((bf16[320,800]{1,0:T(8,128)(2,1)}, bf16[320,800]{1,0:T(8,128)(2,1)S(1)}, u32[]{:S(2)}, u32[]{:S(2)}) %collective-permute-start.53) | collective-permute-done | bytes 512032 | tf_op jit(solution)/shard_map/ppermute | solution.py:167
  659.4 25.6 %collective-permute-done.55 = bf16[640,800]{0,1:T(8,128)(2,1)} collective-permute-done((bf16[640,800]{0,1:T(8,128)(2,1)}, bf16[640,800]{0,1:T(8,128)(2,1)}, u32[]{:S(2)}, u32[]{:S(2)}) %collective-permute-start.55) | collective-permute-done | bytes 1024032 | tf_op jit(solution)/shard_map/ppermute | solution.py:167
  720.2 11.0 multiply_convert_fusion.4
  780.1 20.2 %collective-permute-done.71 = bf16[1280,800]{0,1:T(8,128)(2,1)} collective-permute-done((bf16[1280,800]{0,1:T(8,128)(2,1)S(1)}, bf16[1280,800]{0,1:T(8,128)(2,1)}, u32[]{:S(2)}, u32[]{:S(2)}) %collective-permute-start.71) | collective-permute-done | bytes 2048032 | tf_op jit(solution)/shard_map/ppermute | solution.py:167
  821.5 36.2 %collective-permute-done.72 = bf16[640,800]{0,1:T(8,128)(2,1)} collective-permute-done((bf16[640,800]{0,1:T(8,128)(2,1)S(1)}, bf16[640,800]{0,1:T(8,128)(2,1)}, u32[]{:S(2)}, u32[]{:S(2)}) %collective-permute-start.72) | collective-permute-done | bytes 1024032 | tf_op jit(solution)/shard_map/ppermute | solution.py:167
  922.5 31.4 %collective-permute-done.75 = bf16[640,800]{0,1:T(8,128)(2,1)} collective-permute-done((bf16[640,800]{0,1:T(8,128)(2,1)}, bf16[640,800]{0,1:T(8,128)(2,1)}, u32[]{:S(2)}, u32[]{:S(2)}) %collective-permute-start.75) | collective-permute-done | bytes 1024032 | tf_op jit(solution)/shard_map/ppermute | solution.py:167
  978.8 11.6 collective-permute-done.81
  1025.4 19.8 %collective-permute-done.64 = bf16[128,2560]{1,0:T(8,128)(2,1)S(1)} collective-permute-done((bf16[128,2560]{1,0:T(8,128)(2,1)S(1)}, bf16[128,2560]{1,0:T(8,128)(2,1)S(1)}, u32[]{:S(2)}, u32[]{:S(2)}) %collective-permute-start.64) | collective-permute-done | bytes 655392 | tf_op jit(solution)/shard_map/ppermute | solution.py:167
  1066.6 34.4 %collective-permute-done.83 = bf16[640,800]{0,1:T(8,128)(2,1)S(1)} collective-permute-done((bf16[640,800]{0,1:T(8,128)(2,1)S(1)}, bf16[640,800]{0,1:T(8,128)(2,1)S(1)}, u32[]{:S(2)}, u32[]{:S(2)}) %collective-permute-start.83) | collective-permute-done | bytes 1024032 | tf_op jit(solution)/shard_map/ppermute | solution.py:167
  1101.0 14.8 all-gather.30.cloned.1.call-done
  1173.8 26.0 %collective-permute-done.89 = bf16[64,2560]{1,0:T(8,128)(2,1)S(1)} collective-permute-done((bf16[64,2560]{1,0:T(8,128)(2,1)S(1)}, bf16[64,2560]{1,0:T(8,128)(2,1)S(1)}, u32[]{:S(2)}, u32[]{:S(2)}) %collective-permute-start.89) | collective-permute-done | bytes 327712 | tf_op jit(solution)/shard_map/ppermute | solution.py:167
  1203.9 24.6 %collective-permute-done.92 = bf16[128,2560]{1,0:T(8,128)(2,1)S(1)} collective-permute-done((bf16[128,2560]{1,0:T(8,128)(2,1)S(1)}, bf16[128,2560]{1,0:T(8,128)(2,1)S(1)}, u32[]{:S(2)}, u32[]{:S(2)}) %collective-permute-start.92) | collective-permute-done | bytes 655392 | tf_op jit(solution)/shard_map/ppermute | solution.py:167
  1288.0 35.3 %collective-permute-done.99 = f32[1,768]{1,0:T(1,128)S(1)} collective-permute-done((f32[1,768]{1,0:T(1,128)S(1)}, f32[1,768]{1,0:T(1,128)S(1)}, u32[]{:S(2)}, u32[]{:S(2)}) %collective-permute-start.99) | collective-permute-done | bytes 3104 | tf_op jit(solution)/shard_map/ppermute | solution.py:167
  1422.1 17.4 %collective-permute-done.105 = bf16[64,1056]{0,1:T(8,128)(2,1)S(1)} collective-permute-done((bf16[64,1056]{0,1:T(8,128)(2,1)S(1)}, bf16[64,1056]{0,1:T(8,128)(2,1)S(1)}, u32[]{:S(2)}, u32[]{:S(2)}) %collective-permute-start.105) | collective-permute-done | bytes 135200 | tf_op jit(solution)/shard_map/ppermute | solution.py:167
  1494.5 39.2 %collective-permute-done.112 = bf16[640,800]{0,1:T(8,128)(2,1)} collective-permute-done((bf16[640,800]{0,1:T(8,128)(2,1)}, bf16[640,800]{0,1:T(8,128)(2,1)}, u32[]{:S(2)}, u32[]{:S(2)}) %collective-permute-start.112) | collective-permute-done | bytes 1024032 | tf_op jit(solution)/shard_map/ppermute | solution.py:167
  1558.7 17.4 %collective-permute-done.129 = bf16[320,800]{1,0:T(8,128)(2,1)} collective-permute-done((bf16[320,800]{1,0:T(8,128)(2,1)}, bf16[320,800]{1,0:T(8,128)(2,1)}, u32[]{:S(2)}, u32[]{:S(2)}) %collective-permute-start.129) | collective-permute-done | bytes 512032 | tf_op jit(solution)/shard_map/ppermute | solution.py:167
  (1668 shorter events, 1089.7 us)
Async XLA Ops:
  7.2 73.1 %all-gather.18.cloned.1.call-start = ((), (), s32[]{:S(2)}) async-start(), calls=%async_computation | async-start | bytes 5898240 | tf_op jit(solution)/shard_map/all_gather | solution.py:271
  21.0 136.5 %all-gather.40.cloned.1.call-start = ((), (), s32[]{:S(2)}) async-start(), calls=%async_computation.11 | async-start | bytes 2506752 | tf_op jit(solution)/shard_map/all_gather | solution.py:271
  90.1 84.6 %collective-permute-start.13 = (bf16[80,1056]{1,0:T(8,128)(2,1)}, bf16[80,1056]{1,0:T(8,128)(2,1)}, u32[]{:S(2)}, u32[]{:S(2)}) collective-permute-start(bf16[80,1056]{1,0:T(8,128)(2,1)} %fusion.235), channel_id=1, source_target_pairs={{0,16},{4,20},{8,24},{12,28},{16,0},{20,4},{24,8},{28,12},{1,17},{... | collective-permute-start | bytes 506888 | tf_op jit(solution)/shard_map/ppermute | solution.py:167
  92.5 82.1 %collective-permute-start.14 = (bf16[80,1056]{1,0:T(8,128)(2,1)}, bf16[80,1056]{1,0:T(8,128)(2,1)}, u32[]{:S(2)}, u32[]{:S(2)}) collective-permute-start(bf16[80,1056]{1,0:T(8,128)(2,1)} %fusion.235), channel_id=1, source_target_pairs={{0,4},{4,0},{8,12},{12,8},{16,20},{20,16},{24,28},{28,24},{1,5},{5... | collective-permute-start | bytes 506888 | tf_op jit(solution)/shard_map/ppermute | solution.py:167
  97.5 120.8 %collective-permute-start.15 = (bf16[640,800]{0,1:T(8,128)(2,1)}, bf16[640,800]{0,1:T(8,128)(2,1)}, u32[]{:S(2)}, u32[]{:S(2)}) collective-permute-start(bf16[640,800]{0,1:T(8,128)(2,1)} %pad_maximum_fusion.10), channel_id=1, source_target_pairs={{0,16},{4,20},{8,24},{12,28},{16,0},{20,4},{24,8},{28,12},{1,17},{... | collective-permute-start | bytes 3072008 | tf_op jit(solution)/shard_map/ppermute | solution.py:167
  98.0 120.3 %collective-permute-start.16 = (bf16[640,800]{0,1:T(8,128)(2,1)}, bf16[640,800]{0,1:T(8,128)(2,1)}, u32[]{:S(2)}, u32[]{:S(2)}) collective-permute-start(bf16[640,800]{0,1:T(8,128)(2,1)} %pad_maximum_fusion.10), channel_id=1, source_target_pairs={{0,4},{4,0},{8,12},{12,8},{16,20},{20,16},{24,28},{28,24},{1,5},{5... | collective-permute-start | bytes 3072008 | tf_op jit(solution)/shard_map/ppermute | solution.py:167
  98.8 258.6 %all-gather.20.cloned.1.call-start = ((), (), s32[]{:S(2)}) async-start(), calls=%async_computation.1 | async-start | bytes 5898240 | tf_op jit(solution)/shard_map/all_gather | solution.py:271
  295.9 133.0 %all-gather.42.cloned.1.call-start = ((), (), s32[]{:S(2)}) async-start(), calls=%async_computation.12 | async-start | bytes 6635520 | tf_op jit(solution)/shard_map/all_gather | solution.py:271
  309.5 203.9 %all-gather.22.cloned.1.call-start = ((), (), s32[]{:S(2)}) async-start(), calls=%async_computation.2 | async-start | bytes 2433024 | tf_op jit(solution)/shard_map/all_gather | solution.py:271
  475.2 71.1 %collective-permute-start.44 = (bf16[320,800]{1,0:T(8,128)(2,1)}, bf16[320,800]{1,0:T(8,128)(2,1)}, u32[]{:S(2)}, u32[]{:S(2)}) collective-permute-start(bf16[320,800]{1,0:T(8,128)(2,1)} %copy.281), channel_id=1, source_target_pairs={{0,8},{4,12},{8,0},{12,4},{16,24},{20,28},{24,16},{28,20},{1,9},{5... | collective-permute-start | bytes 1536008 | tf_op jit(solution)/shard_map/ppermute | solution.py:167
  481.2 65.1 %collective-permute-start.42 = (bf16[640,800]{0,1:T(8,128)(2,1)}, bf16[640,800]{0,1:T(8,128)(2,1)}, u32[]{:S(2)}, u32[]{:S(2)}) collective-permute-start(bf16[640,800]{0,1:T(8,128)(2,1)} %pad_maximum_fusion.13), channel_id=1, source_target_pairs={{0,16},{4,20},{8,24},{12,28},{16,0},{20,4},{24,8},{28,12},{1,17},{... | collective-permute-start | bytes 3072008 | tf_op jit(solution)/shard_map/ppermute | solution.py:167
  483.0 63.4 %collective-permute-start.43 = (bf16[640,800]{0,1:T(8,128)(2,1)}, bf16[640,800]{0,1:T(8,128)(2,1)}, u32[]{:S(2)}, u32[]{:S(2)}) collective-permute-start(bf16[640,800]{0,1:T(8,128)(2,1)} %pad_maximum_fusion.13), channel_id=1, source_target_pairs={{0,4},{4,0},{8,12},{12,8},{16,20},{20,16},{24,28},{28,24},{1,5},{5... | collective-permute-start | bytes 3072008 | tf_op jit(solution)/shard_map/ppermute | solution.py:167
  483.5 201.5 %all-gather.24.cloned.1.call-start = ((), (), s32[]{:S(2)}) async-start(), calls=%async_computation.3 | async-start | bytes 5898240 | tf_op jit(solution)/shard_map/all_gather | solution.py:271
  629.0 91.3 %all-gather.26.cloned.1.call-start = ((), (), s32[]{:S(2)}) async-start(), calls=%async_computation.4 | async-start | bytes 5898240 | tf_op jit(solution)/shard_map/all_gather | solution.py:271
  633.4 224.2 %all-gather.28.cloned.1.call-start = ((), (), s32[]{:S(2)}) async-start(), calls=%async_computation.5 | async-start | bytes 5898240 | tf_op jit(solution)/shard_map/all_gather | solution.py:271
  802.2 259.3 %all-gather.34.cloned.1.call-start = ((), (), s32[]{:S(2)}) async-start(), calls=%async_computation.8 | async-start | bytes 2433024 | tf_op jit(solution)/shard_map/all_gather | solution.py:271
  908.7 81.7 %collective-permute-start.82 = (bf16[1280,800]{0,1:T(8,128)(2,1)}, bf16[1280,800]{0,1:T(8,128)(2,1)}, u32[]{:S(2)}, u32[]{:S(2)}) collective-permute-start(bf16[1280,800]{0,1:T(8,128)(2,1)} %convolution_convert_fusion.18), channel_id=1, source_target_pairs={{0,4},{4,0},{8,12},{12,8},{16,20},{20,16},{24,28},{28,24},{1,5},{5... | collective-permute-start | bytes 6144008 | tf_op jit(solution)/shard_map/ppermute | solution.py:167
  992.1 71.5 %all-gather.32.cloned.1.call-start = ((), (), s32[]{:S(2)}) async-start(), calls=%async_computation.7 | async-start | bytes 5898240 | tf_op jit(solution)/shard_map/all_gather | solution.py:271
  992.7 123.1 %all-gather.30.cloned.1.call-start = ((), (), s32[]{:S(2)}) async-start(), calls=%async_computation.6 | async-start | bytes 5898240 | tf_op jit(solution)/shard_map/all_gather | solution.py:271
  1049.0 188.9 %all-gather.44.cloned.1.call-start = ((), (), s32[]{:S(2)}) async-start(), calls=%async_computation.13 | async-start | bytes 6635520 | tf_op jit(solution)/shard_map/all_gather | solution.py:271
  1156.1 172.7 %all-gather.36.cloned.1.call-start = ((), (), s32[]{:S(2)}) async-start(), calls=%async_computation.9 | async-start | bytes 5898240 | tf_op jit(solution)/shard_map/all_gather | solution.py:271
  1234.5 348.0 %all-gather.38.cloned.1.call-start = ((), (), s32[]{:S(2)}) async-start(), calls=%async_computation.10 | async-start | bytes 2433024 | tf_op jit(solution)/shard_map/all_gather | solution.py:271
  1385.1 69.2 %collective-permute-start.109 = (bf16[640,800]{0,1:T(8,128)(2,1)}, bf16[640,800]{0,1:T(8,128)(2,1)}, u32[]{:S(2)}, u32[]{:S(2)}) collective-permute-start(bf16[640,800]{0,1:T(8,128)(2,1)} %split.1052), channel_id=1, source_target_pairs={{0,16},{4,20},{8,24},{12,28},{16,0},{20,4},{24,8},{28,12},{1,17},{... | collective-permute-start | bytes 3072008 | tf_op jit(solution)/shard_map/ppermute | solution.py:167
  1388.4 65.9 %collective-permute-start.110 = (bf16[1280,800]{0,1:T(8,128)(2,1)}, bf16[1280,800]{0,1:T(8,128)(2,1)}, u32[]{:S(2)}, u32[]{:S(2)}) collective-permute-start(bf16[1280,800]{0,1:T(8,128)(2,1)} %convolution_convert_fusion.12), channel_id=1, source_target_pairs={{0,4},{4,0},{8,12},{12,8},{16,20},{20,16},{24,28},{28,24},{1,5},{5... | collective-permute-start | bytes 6144008 | tf_op jit(solution)/shard_map/ppermute | solution.py:167
  (497 other events, 6833.8 us)
Sparse Core Ops, SparseCore 0:
  21.1 49.8 all-gather.17
  98.9 28.5 all-gather.39
  296.0 61.2 all-gather.19
  359.4 35.2 all-gather.41
  483.7 29.7 all-gather.21
  629.1 51.7 all-gather.23
  682.5 33.8 all-gather.25
  802.3 51.3 all-gather.27
  992.2 26.3 all-gather.33
  1020.1 43.4 all-gather.31
  1065.8 49.9 all-gather.29
  1156.2 69.9 all-gather.43
  1234.7 34.0 all-gather.35
  1488.3 28.6 all-gather.37

commit v2 on v1

--- a/solution.py
+++ b/solution.py
@@ -35,6 +35,7 @@
     "u1": (6, 7, 11, 12, 13),
     "d1": (6, 7, 12, 13, 14),
     "w0": (12, 13, 14, 15),
+    "out": (16, 17, 19, 20),
     "grad d1": (15, 16, 17, 18),
     "grad g1": (16, 17, 18, 19),
     "grad u1": (17, 19, 21, 22),
@@ -43,8 +44,10 @@
     "grad gains1": (20, 21, 22, 23, 24),
     "grad d0": (22, 23, 24, 25),
     "grad g0": (23, 24, 26, 27),
-    "grad u0": (24, 26, 27),
-    "grad a0": (26, 27),
+    "grad u0": (24, 26, 28, 29),
+    "grad a0": (26, 28, 30, 31),
+    "grad s0": (28, 29, 30, 31, 32, 33),
+    "grad gains0": (28, 29, 30, 31, 32, 33),
 }
 
 PAIR = 2
@@ -308,6 +311,25 @@
         )
         across = self.swap(across, "tensor", 2)
         along = self.swap(along, "dp", PAIR)
+        return rows.astype(f32) + across.astype(f32) + along.astype(f32)
+
+    def scatter_steps(self, own, other):
+        count = own.shape[0] // 4
+        half = count // 2
+        (taken,) = yield [(other, "tensor", 1)]
+        total = (own.astype(f32) + taken.astype(f32)).astype(bf16)
+        rows, across, along = total[:count], total[count : 2 * count], total[2 * count : 3 * count]
+        first, second = yield [
+            (total[3 * count : 3 * count + half], "dp", PAIR),
+            (total[3 * count + half :], "tensor", 2),
+        ]
+        across = jnp.concatenate(
+            [(across[:half].astype(f32) + first.astype(f32)).astype(bf16), across[half:]], axis=0
+        )
+        along = jnp.concatenate(
+            [along[:half], (along[half:].astype(f32) + second.astype(f32)).astype(bf16)], axis=0
+        )
+        across, along = yield [(across, "tensor", 2), (along, "dp", PAIR)]
         return rows.astype(f32) + across.astype(f32) + along.astype(f32)
 
     def own_rows(self, rows):
@@ -450,9 +472,15 @@
     hidden = flow.tick(hidden)
     down_t = flow.result(f"d{layer}")
     hidden_own, hidden_other = place.relative_rows(hidden)
-    result = middle + residual_scale * place.scatter_rows(
-        dot(hidden_own, down_t, 1, 1).astype(bf16), dot(hidden_other, down_t, 1, 1).astype(bf16)
-    )
+    parts = (
+        dot(hidden_own, down_t, 1, 1).astype(bf16),
+        dot(hidden_other, down_t, 1, 1).astype(bf16),
+    )
+    if layer < LAYERS - 1:
+        result = middle + residual_scale * place.scatter_rows(*parts)
+    else:
+        flow.add("out", place.scatter_steps(*parts))
+        result = middle
     stored = (
         q_low,
         kv_low,
@@ -814,6 +842,9 @@
             allowed,
             gains[layer],
         )
+    for _ in range(28, 34):
+        grad_rows = flow.tick(grad_rows)
+    current = current + residual_scale * flow.result("out")
     layer_grads = []
     for layer in range(LAYERS):
         grad_q_down, grad_kv_down = (a.astype(f32) for a in flow.result(f"grad s{layer}"))

time: 1650 us -> 1630 us (0.988)
  waiting for transfers between devices: 685 us -> 660 us
    ppermute x130, waiting for transfers between devices: 646 us -> 556 us  [swap(): return lax.ppermute(array, axis, [(i, i ^ bit) for i in range(size)])]
    all_gather x14, waiting for transfers between devices: 38.5 us -> 103 us  [gather_rows(): lax.all_gather(rows, ('dp', 'tensor'), axis=0, tiled=tiled, axis_index_gr...]
    unnamed x772 -> x838, local copies, waits for them, and re-layouts: 99.5 us -> 97.6 us
  transfers between devices with their start and end apart: 144 -> 144, of which waited for: 63 -> 62; matrix products, arithmetic and copies ran while one was open for 36% -> 37% of each run, Pallas kernels for 0% -> 0%
where the time goes in v2:
time: 1630 us; the launch traced here: 1610 us
  waiting for transfers between devices  660 us (40%)
  local copies, waits for them, and re-layouts  304 us (19%)
  matrix products  277 us (17%)
  other arithmetic  218 us (13%)
  starting transfers between devices  136 us (8%)
  between operations  20.6 us (1%)
    ppermute x130, waiting for transfers between devices, swap(): return lax.ppermute(array, axis, [(i, i ^ bit) for i in range(size)])  556 us
    dot_general x58, matrix products, dot(): lax.dot_general(left, right, (((left_dim,), (right_dim,)), ((), ())), pre...  237 us
    ppermute x130, starting transfers between devices, swap(): return lax.ppermute(array, axis, [(i, i ^ bit) for i in range(size)])  135 us
    all_gather x14, waiting for transfers between devices, gather_rows(): lax.all_gather(rows, ('dp', 'tensor'), axis=0, tiled=tiled, axis_index_gr...  103 us
    unnamed x838, local copies, waits for them, and re-layouts  97.6 us
    concatenate x9, local copies, waits for them, and re-layouts, gather_weight(): return jnp.concatenate(pieces, axis=0)  48.6 us
  transfers between devices with their start and end apart: 144, of which 62 were waited for; matrix products, arithmetic and copies ran while one was open for 37% of the time, Pallas kernels for 0%

profile of v2, /device:TPU:0, one launch (start us, length us, event | category | flops | bytes accessed | tf_op | source)
XLA Modules:
  0.0 1614.5 jit_solution(3608739633234877815)
XLA Ops:
  63.6 13.1 collective-permute-done.6
  107.9 29.3 %collective-permute-done.12 = bf16[576,640]{1,0:T(8,128)(2,1)S(1)} collective-permute-done((bf16[576,640]{1,0:T(8,128)(2,1)}, bf16[576,640]{1,0:T(8,128)(2,1)S(1)}, u32[]{:S(2)}, u32[]{:S(2)}) %collective-permute-start.12) | collective-permute-done | bytes 737312 | tf_op jit(solution)/shard_map/ppermute | solution.py:170
  253.2 13.9 collective-permute-done.23
  268.9 22.5 %collective-permute-done.27 = bf16[320,800]{1,0:T(8,128)(2,1)S(1)} collective-permute-done((bf16[320,800]{1,0:T(8,128)(2,1)}, bf16[320,800]{1,0:T(8,128)(2,1)S(1)}, u32[]{:S(2)}, u32[]{:S(2)}) %collective-permute-start.27) | collective-permute-done | bytes 512032 | tf_op jit(solution)/shard_map/ppermute | solution.py:170
  317.4 29.0 %collective-permute-done.31 = bf16[288,640]{1,0:T(8,128)(2,1)} collective-permute-done((bf16[288,640]{1,0:T(8,128)(2,1)}, bf16[288,640]{1,0:T(8,128)(2,1)}, u32[]{:S(2)}, u32[]{:S(2)}) %collective-permute-start.31) | collective-permute-done | bytes 368672 | tf_op jit(solution)/shard_map/ppermute | solution.py:170
  346.4 11.2 all-gather.20.cloned.1.call-done
  501.7 12.2 all-gather.22.cloned.1.call-done
  586.4 14.8 collective-permute-done.49
  603.8 20.2 %collective-permute-done.53 = bf16[320,800]{1,0:T(8,128)(2,1)S(1)} collective-permute-done((bf16[320,800]{1,0:T(8,128)(2,1)}, bf16[320,800]{1,0:T(8,128)(2,1)S(1)}, u32[]{:S(2)}, u32[]{:S(2)}) %collective-permute-start.53) | collective-permute-done | bytes 512032 | tf_op jit(solution)/shard_map/ppermute | solution.py:170
  659.9 25.5 %collective-permute-done.55 = bf16[640,800]{0,1:T(8,128)(2,1)} collective-permute-done((bf16[640,800]{0,1:T(8,128)(2,1)}, bf16[640,800]{0,1:T(8,128)(2,1)}, u32[]{:S(2)}, u32[]{:S(2)}) %collective-permute-start.55) | collective-permute-done | bytes 1024032 | tf_op jit(solution)/shard_map/ppermute | solution.py:170
  721.1 11.0 multiply_convert_fusion.4
  779.8 21.9 %collective-permute-done.66 = bf16[1280,800]{0,1:T(8,128)(2,1)} collective-permute-done((bf16[1280,800]{0,1:T(8,128)(2,1)S(1)}, bf16[1280,800]{0,1:T(8,128)(2,1)}, u32[]{:S(2)}, u32[]{:S(2)}) %collective-permute-start.66) | collective-permute-done | bytes 2048032 | tf_op jit(solution)/shard_map/ppermute | solution.py:170
  827.3 39.3 %collective-permute-done.68 = bf16[640,800]{0,1:T(8,128)(2,1)} collective-permute-done((bf16[640,800]{0,1:T(8,128)(2,1)S(1)}, bf16[640,800]{0,1:T(8,128)(2,1)}, u32[]{:S(2)}, u32[]{:S(2)}) %collective-permute-start.68) | collective-permute-done | bytes 1024032 | tf_op jit(solution)/shard_map/ppermute | solution.py:170
  938.5 26.6 %collective-permute-done.71 = bf16[640,800]{0,1:T(8,128)(2,1)} collective-permute-done((bf16[640,800]{0,1:T(8,128)(2,1)}, bf16[640,800]{0,1:T(8,128)(2,1)}, u32[]{:S(2)}, u32[]{:S(2)}) %collective-permute-start.71) | collective-permute-done | bytes 1024032 | tf_op jit(solution)/shard_map/ppermute | solution.py:170
  1013.8 11.0 collective-permute-done.81
  1043.4 44.5 %all-gather.32.cloned.1.call-done = bf16[1024,2560]{1,0:T(8,128)(2,1)} async-done(((bf16[128,2560]{1,0:T(8,128)(2,1)}), bf16[1024,2560]{1,0:T(8,128)(2,1)}) %all-gather.32.cloned.1.call-update) | async-done | bytes 5242896 | tf_op jit(solution)/shard_map/all_gather | solution.py:274
  1090.9 32.8 %all-gather.30.cloned.1.call-done = bf16[1024,2560]{1,0:T(8,128)(2,1)} async-done(((bf16[128,2560]{1,0:T(8,128)(2,1)}), bf16[1024,2560]{1,0:T(8,128)(2,1)}) %all-gather.30.cloned.1.call-update) | async-done | bytes 5242896 | tf_op jit(solution)/shard_map/all_gather | solution.py:274
  1131.9 11.0 multiply_convert_fusion.2
  1181.3 25.5 %collective-permute-done.89 = bf16[64,2560]{1,0:T(8,128)(2,1)S(1)} collective-permute-done((bf16[64,2560]{1,0:T(8,128)(2,1)S(1)}, bf16[64,2560]{1,0:T(8,128)(2,1)S(1)}, u32[]{:S(2)}, u32[]{:S(2)}) %collective-permute-start.89) | collective-permute-done | bytes 327712 | tf_op jit(solution)/shard_map/ppermute | solution.py:170
  1210.9 24.4 %collective-permute-done.92 = bf16[128,2560]{1,0:T(8,128)(2,1)S(1)} collective-permute-done((bf16[128,2560]{1,0:T(8,128)(2,1)S(1)}, bf16[128,2560]{1,0:T(8,128)(2,1)S(1)}, u32[]{:S(2)}, u32[]{:S(2)}) %collective-permute-start.92) | collective-permute-done | bytes 655392 | tf_op jit(solution)/shard_map/ppermute | solution.py:170
  1294.0 35.3 %collective-permute-done.99 = f32[1,768]{1,0:T(1,128)S(1)} collective-permute-done((f32[1,768]{1,0:T(1,128)S(1)}, f32[1,768]{1,0:T(1,128)S(1)}, u32[]{:S(2)}, u32[]{:S(2)}) %collective-permute-start.99) | collective-permute-done | bytes 3104 | tf_op jit(solution)/shard_map/ppermute | solution.py:170
  1424.9 14.9 collective-permute-done.105
  1501.6 14.3 collective-permute-done.112
  1549.9 16.4 %collective-permute-done.118 = bf16[640,132]{0,1:T(8,128)(2,1)S(1)} collective-permute-done((bf16[640,132]{0,1:T(8,128)(2,1)S(1)}, bf16[640,132]{0,1:T(8,128)(2,1)S(1)}, u32[]{:S(2)}, u32[]{:S(2)}) %collective-permute-start.118) | collective-permute-done | bytes 168992 | tf_op jit(solution)/shard_map/ppermute | solution.py:170
  (1738 shorter events, 1073.2 us)
Async XLA Ops:
  7.2 73.1 %all-gather.18.cloned.1.call-start = ((), (), s32[]{:S(2)}) async-start(), calls=%async_computation | async-start | bytes 5898240 | tf_op jit(solution)/shard_map/all_gather | solution.py:274
  21.0 136.6 %all-gather.40.cloned.1.call-start = ((), (), s32[]{:S(2)}) async-start(), calls=%async_computation.11 | async-start | bytes 2506752 | tf_op jit(solution)/shard_map/all_gather | solution.py:274
  90.1 84.6 %collective-permute-start.13 = (bf16[80,1056]{1,0:T(8,128)(2,1)}, bf16[80,1056]{1,0:T(8,128)(2,1)}, u32[]{:S(2)}, u32[]{:S(2)}) collective-permute-start(bf16[80,1056]{1,0:T(8,128)(2,1)} %fusion.235), channel_id=1, source_target_pairs={{0,16},{4,20},{8,24},{12,28},{16,0},{20,4},{24,8},{28,12},{1,17},{... | collective-permute-start | bytes 506888 | tf_op jit(solution)/shard_map/ppermute | solution.py:170
  92.6 82.1 %collective-permute-start.14 = (bf16[80,1056]{1,0:T(8,128)(2,1)}, bf16[80,1056]{1,0:T(8,128)(2,1)}, u32[]{:S(2)}, u32[]{:S(2)}) collective-permute-start(bf16[80,1056]{1,0:T(8,128)(2,1)} %fusion.235), channel_id=1, source_target_pairs={{0,4},{4,0},{8,12},{12,8},{16,20},{20,16},{24,28},{28,24},{1,5},{5... | collective-permute-start | bytes 506888 | tf_op jit(solution)/shard_map/ppermute | solution.py:170
  97.6 121.0 %collective-permute-start.15 = (bf16[640,800]{0,1:T(8,128)(2,1)}, bf16[640,800]{0,1:T(8,128)(2,1)}, u32[]{:S(2)}, u32[]{:S(2)}) collective-permute-start(bf16[640,800]{0,1:T(8,128)(2,1)} %pad_maximum_fusion.10), channel_id=1, source_target_pairs={{0,16},{4,20},{8,24},{12,28},{16,0},{20,4},{24,8},{28,12},{1,17},{... | collective-permute-start | bytes 3072008 | tf_op jit(solution)/shard_map/ppermute | solution.py:170
  98.0 120.5 %collective-permute-start.16 = (bf16[640,800]{0,1:T(8,128)(2,1)}, bf16[640,800]{0,1:T(8,128)(2,1)}, u32[]{:S(2)}, u32[]{:S(2)}) collective-permute-start(bf16[640,800]{0,1:T(8,128)(2,1)} %pad_maximum_fusion.10), channel_id=1, source_target_pairs={{0,4},{4,0},{8,12},{12,8},{16,20},{20,16},{24,28},{28,24},{1,5},{5... | collective-permute-start | bytes 3072008 | tf_op jit(solution)/shard_map/ppermute | solution.py:170
  98.9 258.8 %all-gather.20.cloned.1.call-start = ((), (), s32[]{:S(2)}) async-start(), calls=%async_computation.1 | async-start | bytes 5898240 | tf_op jit(solution)/shard_map/all_gather | solution.py:274
  296.2 133.0 %all-gather.42.cloned.1.call-start = ((), (), s32[]{:S(2)}) async-start(), calls=%async_computation.12 | async-start | bytes 6635520 | tf_op jit(solution)/shard_map/all_gather | solution.py:274
  309.9 204.0 %all-gather.22.cloned.1.call-start = ((), (), s32[]{:S(2)}) async-start(), calls=%async_computation.2 | async-start | bytes 2433024 | tf_op jit(solution)/shard_map/all_gather | solution.py:274
  475.6 71.2 %collective-permute-start.44 = (bf16[320,800]{1,0:T(8,128)(2,1)}, bf16[320,800]{1,0:T(8,128)(2,1)}, u32[]{:S(2)}, u32[]{:S(2)}) collective-permute-start(bf16[320,800]{1,0:T(8,128)(2,1)} %copy.281), channel_id=1, source_target_pairs={{0,8},{4,12},{8,0},{12,4},{16,24},{20,28},{24,16},{28,20},{1,9},{5... | collective-permute-start | bytes 1536008 | tf_op jit(solution)/shard_map/ppermute | solution.py:170
  481.7 65.1 %collective-permute-start.42 = (bf16[640,800]{0,1:T(8,128)(2,1)}, bf16[640,800]{0,1:T(8,128)(2,1)}, u32[]{:S(2)}, u32[]{:S(2)}) collective-permute-start(bf16[640,800]{0,1:T(8,128)(2,1)} %pad_maximum_fusion.13), channel_id=1, source_target_pairs={{0,16},{4,20},{8,24},{12,28},{16,0},{20,4},{24,8},{28,12},{1,17},{... | collective-permute-start | bytes 3072008 | tf_op jit(solution)/shard_map/ppermute | solution.py:170
  483.9 201.4 %all-gather.24.cloned.1.call-start = ((), (), s32[]{:S(2)}) async-start(), calls=%async_computation.3 | async-start | bytes 5898240 | tf_op jit(solution)/shard_map/all_gather | solution.py:274
  629.5 91.6 %all-gather.26.cloned.1.call-start = ((), (), s32[]{:S(2)}) async-start(), calls=%async_computation.4 | async-start | bytes 5898240 | tf_op jit(solution)/shard_map/all_gather | solution.py:274
  633.9 232.8 %all-gather.28.cloned.1.call-start = ((), (), s32[]{:S(2)}) async-start(), calls=%async_computation.5 | async-start | bytes 5898240 | tf_op jit(solution)/shard_map/all_gather | solution.py:274
  804.1 237.5 %all-gather.34.cloned.1.call-start = ((), (), s32[]{:S(2)}) async-start(), calls=%async_computation.8 | async-start | bytes 2433024 | tf_op jit(solution)/shard_map/all_gather | solution.py:274
  925.4 65.0 %collective-permute-start.77 = (bf16[64,2560]{1,0:T(8,128)(2,1)}, bf16[64,2560]{1,0:T(8,128)(2,1)}, u32[]{:S(2)}, u32[]{:S(2)}) collective-permute-start(bf16[64,2560]{1,0:T(8,128)(2,1)} %get-tuple-element.524), channel_id=1, source_target_pairs={{0,8},{4,12},{8,0},{12,4},{16,24},{20,28},{24,16},{28,20},{1,9},{5... | collective-permute-start | bytes 983048 | tf_op jit(solution)/shard_map/ppermute | solution.py:170
  925.4 65.0 %collective-permute-start.78 = (bf16[64,2560]{1,0:T(8,128)(2,1)}, bf16[64,2560]{1,0:T(8,128)(2,1)}, u32[]{:S(2)}, u32[]{:S(2)}) collective-permute-start(bf16[64,2560]{1,0:T(8,128)(2,1)} %get-tuple-element.523), channel_id=1, source_target_pairs={{0,2},{1,3},{2,0},{3,1},{4,6},{5,7},{6,4},{7,5},{8,10},{9,11},{10,... | collective-permute-start | bytes 983048 | tf_op jit(solution)/shard_map/ppermute | solution.py:170
  925.8 75.0 %collective-permute-start.80 = (bf16[1280,800]{0,1:T(8,128)(2,1)}, bf16[1280,800]{0,1:T(8,128)(2,1)}, u32[]{:S(2)}, u32[]{:S(2)}) collective-permute-start(bf16[1280,800]{0,1:T(8,128)(2,1)} %convolution_convert_fusion.18), channel_id=1, source_target_pairs={{0,4},{4,0},{8,12},{12,8},{16,20},{20,16},{24,28},{28,24},{1,5},{5... | collective-permute-start | bytes 6144008 | tf_op jit(solution)/shard_map/ppermute | solution.py:170
  1002.9 85.0 %all-gather.32.cloned.1.call-start = ((), (), s32[]{:S(2)}) async-start(), calls=%async_computation.7 | async-start | bytes 5898240 | tf_op jit(solution)/shard_map/all_gather | solution.py:274
  1003.5 120.2 %all-gather.30.cloned.1.call-start = ((), (), s32[]{:S(2)}) async-start(), calls=%async_computation.6 | async-start | bytes 5898240 | tf_op jit(solution)/shard_map/all_gather | solution.py:274
  1027.7 216.4 %all-gather.44.cloned.1.call-start = ((), (), s32[]{:S(2)}) async-start(), calls=%async_computation.13 | async-start | bytes 6635520 | tf_op jit(solution)/shard_map/all_gather | solution.py:274
  1162.6 172.5 %all-gather.36.cloned.1.call-start = ((), (), s32[]{:S(2)}) async-start(), calls=%async_computation.9 | async-start | bytes 5898240 | tf_op jit(solution)/shard_map/all_gather | solution.py:274
  1241.3 255.5 %all-gather.38.cloned.1.call-start = ((), (), s32[]{:S(2)}) async-start(), calls=%async_computation.10 | async-start | bytes 2433024 | tf_op jit(solution)/shard_map/all_gather | solution.py:274
  1385.5 67.5 %collective-permute-start.109 = (bf16[640,800]{0,1:T(8,128)(2,1)}, bf16[640,800]{0,1:T(8,128)(2,1)}, u32[]{:S(2)}, u32[]{:S(2)}) collective-permute-start(bf16[640,800]{0,1:T(8,128)(2,1)} %split.1052), channel_id=1, source_target_pairs={{0,16},{4,20},{8,24},{12,28},{16,0},{20,4},{24,8},{28,12},{1,17},{... | collective-permute-start | bytes 3072008 | tf_op jit(solution)/shard_map/ppermute | solution.py:170
  (530 other events, 7321.0 us)
Sparse Core Ops, SparseCore 0:
  21.1 49.8 all-gather.17
  99.0 28.5 all-gather.39
  296.3 61.3 all-gather.19
  359.8 35.1 all-gather.41
  484.0 29.8 all-gather.21
  629.6 52.0 all-gather.23
  683.4 33.5 all-gather.25
  804.2 43.4 all-gather.27
  1003.0 28.5 all-gather.33
  1033.1 54.7 all-gather.31
  1090.1 33.5 all-gather.29
  1162.7 70.4 all-gather.43
  1241.5 34.0 all-gather.35
  1464.1 32.6 all-gather.37
